TPU v7x, 512 devices: a whole 4x8x8 slice. The times are simulated.
512 devices in a mesh: ctx: 32 (over y, x), head: 16 (over z, core).
Axes of the slice: x: 4, y: 8, z: 8, core: 2. Of those that a mesh axis runs over, the one named last changes fastest.
Arguments:
- tokens_x: bfloat16 [16384, 8192], P('ctx', 'head'), may hold values from -121 to 121
- raw_dt: float32 [128, 16384], P('head', 'ctx'), may hold values from -4 to 4
- in_b: bfloat16 [16384, 128], P('ctx'), may hold values from -0.5 to 0.5
- in_c: bfloat16 [16384, 128], P('ctx'), may hold values from -0.5 to 0.5
- decay_rate: float32 [128], P('head'), may hold values from 1.2207031e-06 to 2
- skip_gain: float32 [128], P('head'), may hold values from 0.5 to 1.5
- step_bias: float32 [128], P('head'), may hold values from -5 to -3
- grad_y: bfloat16 [16384, 8192], P('ctx', 'head'), may hold values from -121 to 121
Outputs:
- grad_x: bfloat16 [16384, 8192], P('ctx', 'head')
- grad_raw_dt: float32 [128, 16384], P('head', 'ctx')
- grad_b: float32 [16384, 128], P('ctx')
- grad_c: float32 [16384, 128], P('ctx')
- grad_rate: float32 [128], P('head')
- grad_skip: float32 [128], P('head')
- grad_bias: float32 [128], P('head')
All inputs are finite; a program needn't handle non-finite values.
Results may differ from a plain program's by a relative error of at most 0.001.
Values sent between devices are 32-bit elements; how exact they have to be, the bound alone decides.
No kernel may reach another device: no remote copies, remote signals or barrier semaphores. Data moves between devices by JAX's collectives and lax.ppermute only.
A program may use at most 64 MiB of HBM per device.

v0:
```python
import jax
import jax.numpy as jnp
from jax import lax
from jax.sharding import PartitionSpec as P

BLOCK = 256


def carried_in(x, axis, combine, identity, reverse):
    peers, place = (lax.axis_size(axis), lax.axis_index(axis))
    everything = jax.tree.map(lambda part: lax.all_gather(part, axis), x)
    start = jax.tree.map(
        lambda part, zero: jnp.broadcast_to(jnp.asarray(zero, part.dtype), part.shape), x, identity
    )

    def hop(k, before):
        at = peers - 1 - k if reverse else k
        reached = at > place if reverse else at < place
        new = combine(before, jax.tree.map(lambda part: part[at], everything))
        return jax.tree.map(lambda a, b: jnp.where(reached, a, b), new, before)

    return lax.fori_loop(0, peers, hop, start)


def layer_forward(values, raw_dt, in_b, in_c, decay_rate, skip_gain, step_bias, start_state):
    token_count, head_count, head_size = values.shape
    state_size = in_b.shape[1]
    block_count = token_count // BLOCK
    step_sizes = jax.nn.softplus(raw_dt + step_bias[:, None])
    log_decay = -decay_rate[:, None] * step_sizes
    x_blocks = values.reshape(block_count, BLOCK, head_count, head_size)
    step_blocks = step_sizes.reshape(head_count, block_count, BLOCK).transpose(1, 0, 2)
    decay_blocks = log_decay.reshape(head_count, block_count, BLOCK).transpose(1, 0, 2)
    b_blocks = in_b.reshape(block_count, BLOCK, state_size)
    c_blocks = in_c.reshape(block_count, BLOCK, state_size)
    positions = jnp.arange(BLOCK)
    causal = positions[:, None] >= positions[None, :]

    def one_block(carry_state, pieces):
        x_block, step_block, decay_block, b_block, c_block = pieces
        cum_decay = jnp.cumsum(decay_block, axis=1)
        scores = jnp.dot(c_block, b_block.T, precision=lax.Precision.HIGHEST)
        log_gap = cum_decay[:, :, None] - cum_decay[:, None, :]
        mixing = jnp.where(causal[None], jnp.exp(jnp.where(causal[None], log_gap, 0.0)), 0.0)
        mixing = mixing * scores[None] * step_block[:, None, :]
        within = jnp.einsum("hts,shp->thp", mixing, x_block, precision=lax.Precision.HIGHEST)
        carried = jnp.einsum("hpn,tn->thp", carry_state, c_block, precision=lax.Precision.HIGHEST)
        carried = carried * jnp.exp(cum_decay).T[:, :, None]
        block_out = within + carried + skip_gain[None, :, None] * x_block
        end_decay = cum_decay[:, -1]
        state_weight = jnp.exp(end_decay[:, None] - cum_decay) * step_block
        weighted = x_block * state_weight.T[:, :, None]
        next_state = jnp.exp(end_decay)[:, None, None] * carry_state
        next_state = next_state + jnp.einsum(
            "shp,sn->hpn", weighted, b_block, precision=lax.Precision.HIGHEST
        )
        return (next_state, block_out)

    final_state, block_outs = lax.scan(
        jax.checkpoint(one_block),
        start_state,
        (x_blocks, step_blocks, decay_blocks, b_blocks, c_blocks),
    )
    return (block_outs.reshape(token_count, head_count, head_size), final_state)


def combine_pair(earlier_pair, later_pair):
    merged_log = earlier_pair[0] + later_pair[0]
    merged_state = jnp.exp(later_pair[0])[:, None, None] * earlier_pair[1] + later_pair[1]
    return (merged_log, merged_state)


def on_device(tokens_x, raw_dt, in_b, in_c, decay_rate, skip_gain, step_bias, grad_y):
    head_count = decay_rate.shape[0]
    token_count = tokens_x.shape[0]
    head_size = tokens_x.shape[1] // head_count
    values = tokens_x.astype(jnp.float32).reshape(token_count, head_count, head_size)
    b_local = in_b.astype(jnp.float32)
    c_local = in_c.astype(jnp.float32)
    cotangent = grad_y.astype(jnp.float32).reshape(token_count, head_count, head_size)
    step_sizes = jax.nn.softplus(raw_dt + step_bias[:, None])
    cum_decay = jnp.cumsum(-decay_rate[:, None] * step_sizes, axis=1)
    span_decay = cum_decay[:, -1]
    state_weight = jnp.exp(span_decay[:, None] - cum_decay) * step_sizes
    local_state = jnp.einsum(
        "thp,tn->hpn", values * state_weight.T[:, :, None], b_local, precision=lax.Precision.HIGHEST
    )
    reach_grad = jnp.einsum(
        "thp,tn->hpn",
        cotangent * jnp.exp(cum_decay).T[:, :, None],
        c_local,
        precision=lax.Precision.HIGHEST,
    )
    neutral = (jnp.zeros_like(span_decay), jnp.zeros_like(local_state))
    carried_logs, incoming = carried_in(
        (span_decay, local_state), "ctx", combine_pair, neutral, False
    )
    returned_logs, outgoing = carried_in(
        (span_decay, reach_grad), "ctx", combine_pair, neutral, True
    )

    def forward(values, raw_dt, b_local, c_local, decay_rate, skip_gain, step_bias):
        return layer_forward(
            values, raw_dt, b_local, c_local, decay_rate, skip_gain, step_bias, incoming
        )

    outputs, pullback = jax.vjp(
        forward, values, raw_dt, b_local, c_local, decay_rate, skip_gain, step_bias
    )
    grad_v, grad_raw, grad_b, grad_c, grad_rate, grad_skip, grad_bias = pullback(
        (cotangent, outgoing)
    )
    grad_b, grad_c = lax.psum((grad_b, grad_c), "head")
    grad_rate, grad_skip, grad_bias = lax.psum((grad_rate, grad_skip, grad_bias), "ctx")
    grad_x = grad_v.reshape(token_count, head_count * head_size).astype(jnp.bfloat16)
    return (grad_x, grad_raw, grad_b, grad_c, grad_rate, grad_skip, grad_bias)


def solution(mesh):
    placed = (
        P("ctx", "head"),
        P("head", "ctx"),
        P("ctx", None),
        P("ctx", None),
        P("head"),
        P("head"),
        P("head"),
        P("ctx", "head"),
    )
    return jax.shard_map(
        on_device,
        mesh=mesh,
        in_specs=placed,
        out_specs=(
            P("ctx", "head"),
            P("head", "ctx"),
            P("ctx", None),
            P("ctx", None),
            P("head"),
            P("head"),
            P("head"),
        ),
        check_vma=False,
    )
```

profile of v0, /device:TPU:1, one launch (start us, length us, event | category | flops | bytes accessed | tf_op | source)
XLA Modules:
  0.0 437.9 jit_solution(11087657948599977132)
XLA Ops:
  8.7 1.1 reduce-window.64
  11.2 1.3 copy.49
  12.6 1.3 fusion.64
  14.4 1.3 fusion.66
  16.5 1.6 reshape_reshape.7
  18.2 1.3 dynamic-slice
  20.3 62.1 %all-reduce.1 = f32[256]{0:T(256)S(1)} all-reduce(f32[256]{0:T(256)S(1)} %dynamic-update-slice), channel_id=2, replica_groups=mesh['ctx'=32,'head'=16] {'ctx'}, use_global_device_ids=true, to_apply=%add.1 | all-reduce | flops 256 | bytes 2048
  83.4 39.5 %all-gather.8.cloned.1.call-done = f32[256,64,128]{2,1,0:T(8,128)} async-done(((f32[8,64,128]{2,1,0:T(8,128)}), f32[256,64,128]{2,1,0:T(8,128)}) %all-gather.8.cloned.1.call-update) | async-done | bytes 8388624 | tf_op jit(solution)/shard_map/all_gather | solution.py:11
  123.0 35.1 %while.71 = (s32[]{:T(128)}, f32[8,64,128]{2,1,0:T(8,128)S(1)}, s32[]{:T(128)}, f32[32,8]{1,0:T(8,128)S(1)}, f32[32,8,64,128]{3,2,1,0:T(8,128)}, /*index=5*/s32[]{:T(128)}, s32[]{:T(128)}) while((s32[]{:T(128)}, f32[8,64,128]{2,1,0:T(8,128)S(1)}, s32[]{:T(128)}, f32[32,8]{1,0:T(8,128)S(1)}, f32[32,8,64,128]{3,2,1,0:T(8,128)}, ...), condition=%wide.region_5.6_spmd.clone, body=%wide.region_4.5_spmd.clone.sunk | while | flops 262148 | bytes 786633 | solution.py:22
  139.4 1.1 fusion.125
  140.5 1.1 fusion.125
  146.0 1.1 fusion.125
  150.4 1.1 fusion.125
  151.5 1.1 fusion.125
  154.8 1.1 fusion.125
  158.0 5.2 %while.69 = (s32[]{:T(128)}, f32[8,64,128]{2,1,0:T(8,128)S(1)}, f32[2,8,64,128]{3,2,1,0:T(8,128)}, f32[2,8,256]{2,1,0:T(8,128)S(1)}, f32[2,256,8,64]{1,3,2,0:T(8...) while((s32[]{:T(128)}, f32[8,64,128]{2,1,0:T(8,128)S(1)}, ...), condition=%wide.region_9.10_spmd, body=%wide.region_6.9_spmd.sunk | while | flops 201855008 | bytes 1788653 | solution.py:59
  163.2 64.6 %all-gather.6.cloned.1.call-done = f32[256,64,128]{2,1,0:T(8,128)} async-done(((f32[8,64,128]{2,1,0:T(8,128)}), f32[256,64,128]{2,1,0:T(8,128)}) %all-gather.6.cloned.1.call-update) | async-done | bytes 8388624 | tf_op jit(solution)/shard_map/all_gather | solution.py:11
  227.8 35.4 %while.70 = (s32[]{:T(128)}, f32[8,64,128]{2,1,0:T(8,128)S(1)}, s32[]{:T(128)}, f32[32,8]{1,0:T(8,128)S(1)}, f32[32,8,64,128]{3,2,1,0:T(8,128)}, /*index=5*/s32[]{:T(128)}, s32[]{:T(128)}, s32[]{:T(128)}, s32[]{:T(128)}) while((s32[]{:T(128)}, f32[8,64,128]{2,1,0:T(8,128)S(1)}, s32[]{:T(128)}, f32[32,8]{1,0:T(8,128)S(1)}, ...), condition=%wide.region_3.4_spmd.clone, body=%wide.region_2.3_spmd.clone.sunk | while | flops 262152 | bytes 786695 | solution.py:22
  228.9 1.1 fusion.124
  230.0 1.1 fusion.124
  231.1 1.1 fusion.124
  232.2 1.1 fusion.124
  233.4 1.1 fusion.124
  236.7 1.1 fusion.124
  240.0 1.1 fusion.124
  248.9 1.1 fusion.124
  257.8 1.1 fusion.124
  261.1 1.1 fusion.124
  266.7 47.0 %while.72 = (s32[]{:T(128)}, f32[8]{0:T(128)}, f32[8,64,128]{2,1,0:T(8,128)S(1)}, bf16[2,256,8,64]{1,3,2,0:T(8,128)(2,1)}, f32[2,8,256]{2,1,0:T(8,128)}, /*index...) while((s32[]{:T(128)}, f32[8]{0:T(128)}, ...), condition=%wide.region_24.25_spmd.clone, body=%wide.region_10.0_spmd.clone.sunk | while | flops 2126997504 | bytes 22467084 | solution.py:59
  266.8 1.8 constant_dynamic-slice_fusion.2
  272.0 4.1 fusion.146
  276.7 1.4 multiply_reduce_fusion.8
  281.1 1.3 fusion.151
  282.4 2.5 reduce-window.80
  285.2 3.8 fusion.150
  290.2 1.8 constant_dynamic-slice_fusion.2
  295.5 4.1 fusion.146
  300.2 1.4 multiply_reduce_fusion.8
  304.6 1.3 fusion.151
  305.9 2.5 reduce-window.80
  308.7 3.8 fusion.150
  313.8 1.6 fusion.75
  315.4 58.3 %all-reduce.2 = (f32[8]{0:T(128)}, f32[8]{0:T(128)}, f32[8]{0:T(128)}) all-reduce(f32[8]{0:T(128)S(1)} %neg.31, f32[8]{0:T(128)} %get-tuple-element.624, f32[8]{0:T(128)S(1)} %get-tuple-element.909), channel_id=1, replica_groups=mesh['ctx'=32,'head'=16] {'ctx'}, use_global_device_ids=true, to_apply=%region_28.29 | all-reduce | flops 24 | bytes 192 | tf_op jit(solution)/shard_map/psum | solution.py:114
  373.6 1.6 copy.55
  375.3 1.4 reshape.330
  376.7 51.4 %all-reduce.6.cloned.1.call-done = (f32[512,128]{1,0:T(8,128)}, f32[512,128]{1,0:T(8,128)}) async-done(((f32[512,128]{1,0:T(8,128)}, f32[512,128]{1,0:T(8,128)}), (f32[512,128]{1,0:T(8,128)}, f32[512,128]{1,0:T(8,128)})) %all-reduce.6.cloned.1.call-update) | async-done | bytes 524304 | tf_op jit(solution)/shard_map/psum | solution.py:113
  428.0 1.7 copy.123
  429.7 1.7 copy.124
  (284 shorter events, 82.0 us)
Async XLA Ops:
  7.2 5.5 %copy-start.4 = (bf16[512,128]{1,0:T(8,128)(2,1)S(1)}, bf16[512,128]{1,0:T(8,128)(2,1)}, u32[]{:S(2)}) copy-start(bf16[512,128]{1,0:T(8,128)(2,1)} %param.18) | copy-start | bytes 393220
  7.2 115.8 %all-gather.8.cloned.1.call-start = ((), (), s32[]{:S(2)}) async-start(), calls=%async_computation.1 | async-start | bytes 8650752 | tf_op jit(solution)/shard_map/all_gather | solution.py:11
  7.9 0.8 copy-start.14
  11.2 2.9 copy-start.6
  12.6 1.8 copy-start.5
  14.0 213.8 %all-gather.6.cloned.1.call-start = ((), (), s32[]{:S(2)}) async-start(), calls=%async_computation | async-start | bytes 8650752 | tf_op jit(solution)/shard_map/all_gather | solution.py:11
  15.8 412.3 %all-reduce.6.cloned.1.call-start = ((), (), s32[]{:S(2)}) async-start(), calls=%async_computation.2 | async-start | bytes 1048576 | tf_op jit(solution)/shard_map/psum | solution.py:113
  266.7 2.9 copy-start.1
  272.0 4.2 copy-start
  272.0 4.1 copy-start.2
  276.5 1.6 copy-start.3
  278.1 6.9 %copy-start.10 = (f32[2,8,256]{2,1,0:T(8,128)S(1)}, f32[2,8,256]{2,1,0:T(8,128)}, u32[]{:S(2)}) copy-start(f32[2,8,256]{2,1,0:T(8,128)} %get-tuple-element.1280) | copy-start | bytes 49156 | tf_op jit(solution)/shard_map/transpose(jvp())/while
  278.1 7.0 %copy-start.7 = (f32[8,256]{1,0:T(8,128)S(1)}, f32[8,256]{1,0:T(8,128)}, u32[]{:S(2)}) copy-start(f32[8,256]{1,0:T(8,128)} %get-tuple-element.1178) | copy-start | bytes 24580 | tf_op jit(solution)/shard_map/transpose(jvp())/while
  278.1 7.0 %copy-start.8 = (f32[2,8,256]{2,1,0:T(8,128)S(1)}, f32[2,8,256]{2,1,0:T(8,128)}, u32[]{:S(2)}) copy-start(f32[2,8,256]{2,1,0:T(8,128)} %get-tuple-element.1279) | copy-start | bytes 49156 | tf_op jit(solution)/shard_map/transpose(jvp())/while
  278.1 7.0 %copy-start.15 = (f32[8]{0:T(128)S(1)}, f32[8]{0:T(128)}, u32[]{:S(2)}) copy-start(f32[8]{0:T(128)} %get-tuple-element.1172) | copy-start | bytes 100 | tf_op jit(solution)/shard_map/transpose(jvp())/while
  285.1 3.9 copy-start.11
  285.2 3.9 copy-start.9
  285.2 4.5 %copy-start.12 = (f32[8]{0:T(128)S(1)}, f32[8]{0:T(128)}, u32[]{:S(2)}) copy-start(f32[8]{0:T(128)} %get-tuple-element.1276) | copy-start | bytes 100 | tf_op jit(solution)/shard_map/transpose(jvp())/while
  289.7 0.5 copy-start.13
  290.2 2.9 copy-start.1
  295.5 4.2 copy-start
  295.5 4.1 copy-start.2
  300.0 1.6 copy-start.3
  301.6 6.9 %copy-start.10 = (f32[2,8,256]{2,1,0:T(8,128)S(1)}, f32[2,8,256]{2,1,0:T(8,128)}, u32[]{:S(2)}) copy-start(f32[2,8,256]{2,1,0:T(8,128)} %get-tuple-element.1280) | copy-start | bytes 49156 | tf_op jit(solution)/shard_map/transpose(jvp())/while
  301.6 7.0 %copy-start.7 = (f32[8,256]{1,0:T(8,128)S(1)}, f32[8,256]{1,0:T(8,128)}, u32[]{:S(2)}) copy-start(f32[8,256]{1,0:T(8,128)} %get-tuple-element.1178) | copy-start | bytes 24580 | tf_op jit(solution)/shard_map/transpose(jvp())/while
  301.6 7.0 %copy-start.8 = (f32[2,8,256]{2,1,0:T(8,128)S(1)}, f32[2,8,256]{2,1,0:T(8,128)}, u32[]{:S(2)}) copy-start(f32[2,8,256]{2,1,0:T(8,128)} %get-tuple-element.1279) | copy-start | bytes 49156 | tf_op jit(solution)/shard_map/transpose(jvp())/while
  301.6 7.0 %copy-start.15 = (f32[8]{0:T(128)S(1)}, f32[8]{0:T(128)}, u32[]{:S(2)}) copy-start(f32[8]{0:T(128)} %get-tuple-element.1172) | copy-start | bytes 100 | tf_op jit(solution)/shard_map/transpose(jvp())/while
  308.6 3.9 copy-start.11
  308.6 3.9 copy-start.9
  308.7 4.5 %copy-start.12 = (f32[8]{0:T(128)S(1)}, f32[8]{0:T(128)}, u32[]{:S(2)}) copy-start(f32[8]{0:T(128)} %get-tuple-element.1276) | copy-start | bytes 100 | tf_op jit(solution)/shard_map/transpose(jvp())/while
  313.2 0.5 copy-start.13
Sparse Core Ops, SparseCore 0:
  14.1 108.7 all-gather.7
  126.7 101.0 all-gather.5
  313.9 114.1 all-reduce.5
where the time goes:
time: 441 us; the launch traced here: 438 us
  waiting for transfers between devices  156 us (35%)
  blocking collectives  120 us (27%)
  other arithmetic  84.5 us (19%)
  matrix products  33.3 us (8%)
  local copies, waits for them, and re-layouts  26.8 us (6%)
  between operations  14.6 us (3%)
    all_gather x2, waiting for transfers between devices, carried_in(): everything = jax.tree.map(lambda part: lax.all_gather(part, axis), x)  104 us
    select_n x64, other arithmetic, hop(): return jax.tree.map(lambda a, b: jnp.where(reached, a, b), new, before)  67.5 us
    unnamed x1, blocking collectives  62.1 us
    psum x1, blocking collectives, on_device(): lax.psum((grad_rate, grad_skip, grad_bias), 'ctx')  58.3 us
    psum x1, waiting for transfers between devices, on_device(): grad_b, grad_c = lax.psum((grad_b, grad_c), 'head')  51.4 us
    dot_general x4, matrix products, one_block(): jnp.einsum('hts,shp->thp', mixing, x_block, precision=lax.Precision.HIGHEST)  15.9 us
    another operation x18, other arithmetic  10.4 us
    unnamed x17, local copies, waits for them, and re-layouts  9.4 us
  transfers between devices with their start and end apart: 3, of which 3 were waited for; matrix products, arithmetic and copies ran while one was open for 11% of the time, Pallas kernels for 0%

commit v1 on v0

v1 whole, which is shorter than its diff:
```python
import functools

import jax
import jax.numpy as jnp
from jax import lax
from jax.experimental import pallas as pl
from jax.experimental.pallas import tpu as pltpu
from jax.sharding import Mesh
from jax.sharding import PartitionSpec as P

F32, BF16 = jnp.float32, jnp.bfloat16
TOK, HEADS, DIM, STATE = 512, 8, 64, 128
COLS = HEADS * DIM
TB = 128
NB = TOK // TB
LOG2E = 1.4426950408889634
NT = (((1,), (1,)), ((), ()))
TN = (((0,), (0,)), ((), ()))
NN = (((1,), (0,)), ((), ()))


def mm(a, b, dims=NN):
    return lax.dot_general(a, b, dims, preferred_element_type=F32)


def split2(a):
    hi = a.astype(BF16)
    return hi, (a - hi.astype(F32)).astype(BF16)


def to_column(row):
    eye = lax.broadcasted_iota(jnp.int32, (HEADS, HEADS), 0) == lax.broadcasted_iota(
        jnp.int32, (HEADS, HEADS), 1
    )
    return jnp.sum(jnp.where(eye, row, 0.0), axis=1, keepdims=True)


def to_row(column):
    lane = lax.broadcasted_iota(jnp.int32, (HEADS, 128), 1)
    sub = lax.broadcasted_iota(jnp.int32, (HEADS, 128), 0)
    return jnp.sum(jnp.where(lane == sub, column, 0.0), axis=0, keepdims=True)


def member():
    lane = lax.broadcasted_iota(jnp.int32, (HEADS, COLS), 1)
    sub = lax.broadcasted_iota(jnp.int32, (HEADS, COLS), 0)
    return lane // DIM == sub


def over_channels(column):
    return jnp.sum(jnp.where(member(), column, 0.0), axis=0, keepdims=True)


def sum_channels(a):
    group = jnp.where(member(), 1.0, 0.0).astype(BF16)
    hi, lo = split2(a)
    return mm(group, hi, NT) + mm(group, lo, NT)


def expand(rows):
    hi = rows.astype(BF16).astype(F32)
    rest = rows - hi
    mid = rest.astype(BF16).astype(F32)
    parts = jnp.concatenate([hi, mid, rest - mid], axis=0).T.astype(BF16)
    lane = lax.broadcasted_iota(jnp.int32, (3 * HEADS, COLS), 1)
    sub = lax.broadcasted_iota(jnp.int32, (3 * HEADS, COLS), 0)
    spread = jnp.where(lane // DIM == lax.rem(sub, HEADS), 1.0, 0.0).astype(BF16)
    return mm(parts, spread)


def softplus(v):
    z = jnp.exp(-jnp.abs(v))
    u = 1.0 + z
    small = jnp.where(u == 1.0, z, jnp.log(u) * (z / jnp.where(u == 1.0, 1.0, u - 1.0)))
    return jnp.maximum(v, 0.0) + small


def decays(raw_ref, rate_ref, bias_ref):
    raw = raw_ref[...] + to_column(bias_ref[...])
    dt = softplus(raw)
    a = -(to_column(rate_ref[...]) * LOG2E) * dt
    stacked = jnp.concatenate([a[:, b * TB : (b + 1) * TB] for b in range(NB)], axis=0)
    s = lax.broadcasted_iota(jnp.int32, (TB, TB), 0)
    t = lax.broadcasted_iota(jnp.int32, (TB, TB), 1)
    upto = jnp.where(s <= t, 1.0, 0.0)
    cum = lax.dot_general(
        stacked, upto, NN, precision=lax.Precision.HIGHEST, preferred_element_type=F32
    )
    cum = [cum[b * HEADS : (b + 1) * HEADS] for b in range(NB)]
    total = [c[:, TB - 1 : TB] for c in cum]
    return raw, dt, cum, total


def head_weights(dt, cum, total):
    v, w = [], []
    for b in range(NB):
        v.append(jnp.exp2(cum[b] + sum(total[:b], jnp.zeros_like(total[0]))))
        rest = total[b] - cum[b] + sum(total[b + 1 :], jnp.zeros_like(total[0]))
        w.append(jnp.exp2(rest))
    return jnp.concatenate(v, axis=1), jnp.concatenate(w, axis=1) * dt


def k_states(
    x_ref, g_ref, b_ref, c_ref, raw_ref, rate_ref, bias_ref, send_ref, state_ref, decay_ref
):
    _, dt, cum, total = decays(raw_ref, rate_ref, bias_ref)
    v, w = head_weights(dt, cum, total)
    xw = split2(x_ref[...].astype(F32) * expand(w))
    gv = split2(g_ref[...].astype(F32) * expand(v))
    b, c = b_ref[...], c_ref[...]
    forward = mm(b, xw[0], TN) + mm(b, xw[1], TN)
    backward = mm(c, gv[0], TN) + mm(c, gv[1], TN)
    state_ref[...] = forward
    end = over_channels(jnp.exp2(sum(total)))
    decay_ref[...] = jnp.broadcast_to(end, (8, COLS))
    pieces = send_ref.shape[0]
    for j in range(pieces):
        source, k = (backward if j % 2 else forward), j // 2
        for q in range(4):
            send_ref[j, q * 8 : q * 8 + 8, :] = source[k * 8 : k * 8 + 8, q * 128 : q * 128 + 128]
            send_ref[j, 32 + q : 33 + q, :] = end[:, q * 128 : q * 128 + 128]
        send_ref[j, 36:40, :] = jnp.zeros((4, 128), F32)


def k_scan(odd_ref, got_ref, out_ref):
    pieces = got_ref.shape[0]
    odd = odd_ref[0]

    def step(i, acc):
        at = jnp.where(odd == 1, pieces - 1 - i, i)
        new = []
        for q in range(4):
            out_ref[at, q * 8 : q * 8 + 8, :] = acc[q]
            new.append(
                acc[q] * got_ref[at, 32 + q : 33 + q, :] + got_ref[at, q * 8 : q * 8 + 8, :]
            )
        return tuple(new)

    lax.fori_loop(0, pieces, step, tuple(jnp.zeros((8, 128), F32) for _ in range(4)))


def k_inner(
    x_ref, g_ref, b_ref, c_ref, raw_ref, rate_ref, bias_ref, skip_ref,
    dx_ref, rs_ref, cs_ref, db_ref, dc_ref, xh_ref, xl_ref, gh_ref, gl_ref, sk_ref,
    score_ref, ds_ref,
):
    _, dt, cum, total = decays(raw_ref, rate_ref, bias_ref)
    v, w = head_weights(dt, cum, total)
    x32, g32 = x_ref[...].astype(F32), g_ref[...].astype(F32)
    xh_ref[...], xl_ref[...] = split2(x32 * expand(w))
    gh_ref[...], gl_ref[...] = split2(g32 * expand(v))
    sk_ref[...] = jnp.broadcast_to(jnp.sum(x32 * g32, axis=0, keepdims=True), (8, COLS))
    score_ref[...] = mm(b_ref[...], c_ref[...], NT)
    rs_ref[...] = jnp.zeros_like(rs_ref)
    log_dt = jnp.log(dt) * LOG2E
    column = (jnp.concatenate(cum, axis=1) - log_dt).T
    s = lax.broadcasted_iota(jnp.int32, (TB, TB), 0)
    t = lax.broadcasted_iota(jnp.int32, (TB, TB), 1)
    causal = s <= t
    row = []
    for sb in range(NB):
        row.append(
            jnp.concatenate(
                [
                    cum[tb] + sum(total[sb:tb], jnp.zeros_like(total[0]))
                    for tb in range(sb, NB)
                ],
                axis=1,
            )
        )
    low = lax.broadcasted_iota(jnp.int32, (1, 128), 1) < DIM
    for pair in range(HEADS // 2):
        lanes = slice(pair * 128, pair * 128 + 128)
        zero = jnp.zeros((), BF16)
        gp = g_ref[:, lanes]
        g_of = (jnp.where(low, gp, zero), jnp.where(low, zero, gp))
        for sb in range(NB):
            at = slice(sb * TB, sb * TB + TB)
            after = slice(sb * TB, TOK)
            xs = x_ref[at, lanes]
            both = jnp.concatenate([jnp.where(low, xs, zero), jnp.where(low, zero, xs)], axis=0)
            q2 = mm(both, gp[after], NT)
            score = score_ref[at, after]
            ds, u = None, None
            for e in range(2):
                h = pair * 2 + e
                q = q2[e * TB : (e + 1) * TB]
                decay = jnp.exp2(row[sb][h : h + 1] - column[at, h : h + 1])
                first = jnp.where(causal, decay[:, :TB], 0.0)
                decay = jnp.concatenate([first, decay[:, TB:]], axis=1) if sb < NB - 1 else first
                part = decay * q
                mix = decay * score
                ds = part if ds is None else ds + part
                rs_ref[h : h + 1, after] += jnp.sum(mix * q, axis=0, keepdims=True)
                u2 = mm(jnp.concatenate(split2(mix), axis=0), g_of[e][after])
                u2 = u2[:TB] + u2[TB:]
                u = u2 if u is None else u + u2
            dx_ref[at, lanes] = u
            if pair == 0:
                ds_ref[at, after] = ds
            else:
                ds_ref[at, after] += ds
    for sb in range(NB):
        at, after = slice(sb * TB, sb * TB + TB), slice(sb * TB, TOK)
        d2 = mm(jnp.concatenate(split2(ds_ref[at, after]), axis=0), c_ref[after, :])
        db_ref[at, :] = d2[:TB] + d2[TB:]
        upto = slice(0, sb * TB + TB)
        hi, lo = split2(ds_ref[upto, at])
        dc_ref[at, :] = mm(hi, b_ref[upto, :], TN) + mm(lo, b_ref[upto, :], TN)
    u = dx_ref[...]
    cs_ref[...] = sum_channels(x32 * u)
    dx_ref[...] = u + g32 * over_channels(to_column(skip_ref[...]))


def join(got_ref, odd):
    return jnp.concatenate(
        [
            jnp.concatenate(
                [got_ref[2 * k + odd, q * 8 : q * 8 + 8, :] for q in range(4)], axis=1
            )
            for k in range(got_ref.shape[0] // 2)
        ],
        axis=0,
    )


def k_proj(core_ref, got_ref, xh_ref, xl_ref, gh_ref, gl_ref, db_ref, dc_ref, keep_ref, send_ref):
    def carried(state, hi_ref, lo_ref):
        sh, sl = split2(state)
        two = mm(hi_ref[...], jnp.concatenate([sh, sl], axis=0), NT)
        return two[:, :STATE] + two[:, STATE:] + mm(lo_ref[...], sh, NT)

    dc = dc_ref[...] + carried(join(got_ref, 0), gh_ref, gl_ref)
    db = db_ref[...] + carried(join(got_ref, 1), xh_ref, xl_ref)
    first = core_ref[0] == 0

    @pl.when(first)
    def _():
        keep_ref[...] = db
        send_ref[...] = dc

    @pl.when(jnp.logical_not(first))
    def _():
        keep_ref[...] = dc
        send_ref[...] = db


def k_close(
    got_ref, x_ref, g_ref, b_ref, c_ref, raw_ref, rate_ref, bias_ref,
    part_ref, rs_ref, cs_ref, state_ref, end_ref, sk_ref,
    dx_ref, draw_ref, param_ref,
):
    raw, dt, cum, total = decays(raw_ref, rate_ref, bias_ref)
    v, w = head_weights(dt, cum, total)
    before, after = join(got_ref, 0), join(got_ref, 1)
    sh, sl = split2(before)
    rh, rl = split2(after)
    carried_y = mm(c_ref[...], sh) + mm(c_ref[...], sl)
    carried_u = mm(b_ref[...], rh) + mm(b_ref[...], rl)
    dx_ref[...] = (part_ref[...] + carried_u * expand(w)).astype(BF16)
    rs = rs_ref[...] + v * sum_channels(g_ref[...].astype(F32) * carried_y)
    cs = cs_ref[...] + w * sum_channels(x_ref[...].astype(F32) * carried_u)
    last = before * end_ref[0:1, :] + state_ref[...]
    tail = jnp.sum(after * last, axis=0, keepdims=True)

    def per_head(row):
        return jnp.sum(jnp.where(member(), row, 0.0), axis=1, keepdims=True)

    dcum = rs - cs
    stacked = jnp.concatenate([dcum[:, b * TB : (b + 1) * TB] for b in range(NB)], axis=0)
    s = lax.broadcasted_iota(jnp.int32, (TB, TB), 0)
    t = lax.broadcasted_iota(jnp.int32, (TB, TB), 1)
    down = lax.dot_general(
        stacked,
        jnp.where(s >= t, 1.0, 0.0),
        NN,
        precision=lax.Precision.HIGHEST,
        preferred_element_type=F32,
    )
    later = per_head(tail)
    da = [None] * NB
    for b in reversed(range(NB)):
        here = down[b * HEADS : (b + 1) * HEADS]
        da[b] = here + later
        later = later + here[:, 0:1]
    da = jnp.concatenate(da, axis=1)
    draw = (cs / dt - da * to_column(rate_ref[...])) * (1.0 / (1.0 + jnp.exp(-raw)))
    draw_ref[...] = draw
    rate = to_row(-jnp.sum(da * dt, axis=1, keepdims=True))
    bias = to_row(jnp.sum(draw, axis=1, keepdims=True))
    skip = to_row(per_head(sk_ref[0:1, :]))
    rows = jnp.concatenate([rate, bias, skip, jnp.zeros((5, 128), F32)], axis=0)
    for j in range(param_ref.shape[0]):
        param_ref[j] = rows


VMEM = pl.BlockSpec(memory_space=pltpu.VMEM)
SMEM = pl.BlockSpec(memory_space=pltpu.SMEM)


def shape(dims, dtype=F32):
    return jax.ShapeDtypeStruct(dims, dtype)


def call(body, name, specs, outs, flops, scratch=()):
    return pl.pallas_call(
        body,
        in_specs=specs,
        out_specs=[VMEM] * len(outs),
        out_shape=outs,
        scratch_shapes=list(scratch),
        compiler_params=pltpu.CompilerParams(vmem_limit_bytes=48 << 20),
        cost_estimate=pl.CostEstimate(flops=flops, bytes_accessed=4 << 20, transcendentals=0),
        name=name,
    )


def states(pieces, *args):
    outs = [shape((pieces, 40, 128)), shape((STATE, COLS)), shape((8, COLS))]
    return call(k_states, "states", [VMEM] * 7, outs, 1 << 31)(*args)


def scan(odd, got):
    out = [shape((got.shape[0], 32, 128))]
    return call(k_scan, "scan", [SMEM, VMEM], out, 1 << 28)(odd, got)[0]


def inner(*args):
    outs = [
        shape((TOK, COLS)), shape((HEADS, TOK)), shape((HEADS, TOK)),
        shape((TOK, STATE)), shape((TOK, STATE)),
        shape((TOK, COLS), BF16), shape((TOK, COLS), BF16),
        shape((TOK, COLS), BF16), shape((TOK, COLS), BF16), shape((8, COLS)),
    ]
    scratch = [pltpu.VMEM((TOK, TOK), F32), pltpu.VMEM((TOK, TOK), F32)]
    return call(k_inner, "inner", [VMEM] * 8, outs, 1 << 33, scratch)(*args)


def proj(*args):
    outs = [shape((TOK, STATE)), shape((TOK, STATE))]
    return call(k_proj, "proj", [SMEM] + [VMEM] * 7, outs, 1 << 30)(*args)


def close(pieces, *args):
    outs = [shape((TOK, COLS), BF16), shape((HEADS, TOK)), shape((pieces, 8, 128))]
    return call(k_close, "close", [VMEM] * 14, outs, 1 << 31)(*args)


def on_device(tokens_x, raw_dt, in_b, in_c, decay_rate, skip_gain, step_bias, grad_y):
    ctx = ("y", "x")
    pieces = lax.axis_size(ctx)
    odd = lax.rem(lax.axis_index(ctx), 2).astype(jnp.int32).reshape(1)
    core = lax.axis_index("c").astype(jnp.int32).reshape(1)
    rate, skip, bias = (a.reshape(1, HEADS) for a in (decay_rate, skip_gain, step_bias))
    data = (tokens_x, grad_y, in_b, in_c, raw_dt, rate, bias)

    send, state, end = states(pieces, *data)
    got = lax.all_to_all(send, ctx, 0, 0)
    part, rs, cs, db, dc, xh, xl, gh, gl, sk = inner(*data, skip)
    got = lax.all_to_all(scan(odd, got), ctx, 0, 0)
    keep, send = proj(core, got, xh, xl, gh, gl, db, dc)
    swap = [(0, 1), (1, 0)]
    mine = keep + lax.ppermute(send, "c", swap)
    grad_x, grad_raw, params = close(pieces, got, *data, part, rs, cs, state, end, sk)
    ranks = lax.axis_size("z")
    mine = lax.all_to_all(mine.reshape(ranks, TOK // ranks, STATE), "z", 0, 0)
    mine = jnp.broadcast_to(jnp.sum(mine, axis=0)[None], mine.shape)
    mine = lax.all_to_all(mine, "z", 0, 0).reshape(TOK, STATE)
    other = lax.ppermute(mine, "c", swap)
    first = core[0] == 0
    grad_b, grad_c = jnp.where(first, mine, other), jnp.where(first, other, mine)
    params = jnp.sum(lax.all_to_all(params, ctx, 0, 0), axis=0)
    return (
        grad_x, grad_raw, grad_b, grad_c,
        params[0, :HEADS], params[2, :HEADS], params[1, :HEADS],
    )


def solution(mesh):
    fine = Mesh(mesh.devices.reshape(8, 4, 8, 2), ("y", "x", "z", "c"))
    ctx, head = ("y", "x"), ("z", "c")
    return jax.shard_map(
        on_device,
        mesh=fine,
        in_specs=(
            P(ctx, head), P(head, ctx), P(ctx, None), P(ctx, None),
            P(head), P(head), P(head), P(ctx, head),
        ),
        out_specs=(
            P(ctx, head), P(head, ctx), P(ctx, None), P(ctx, None),
            P(head), P(head), P(head),
        ),
        check_vma=False,
    )
```

time: 441 us -> 124 us (0.28)
  the two profiles are of different devices: /device:TPU:1 before, /device:TPU:8 now
where the time goes in v1:
time: 124 us; the launch traced here: 123 us
  waiting for transfers between devices  44.8 us (36%)
  starting transfers between devices  28.2 us (23%)
  blocking collectives  22.4 us (18%)
  local copies, waits for them, and re-layouts  14 us (11%)
  Pallas kernels  11.5 us (9%)
    all_to_all x1, blocking collectives, on_device(): mine = lax.all_to_all(mine.reshape(ranks, TOK // ranks, STATE), 'z', 0, 0)  22.4 us
    all_to_all x1, waiting for transfers between devices, on_device(): got = lax.all_to_all(send, ctx, 0, 0)  19.8 us
    unnamed x46, local copies, waits for them, and re-layouts  12.7 us
    all_to_all x1, starting transfers between devices, on_device(): got = lax.all_to_all(send, ctx, 0, 0)  10.2 us
    all_to_all x1, waiting for transfers between devices, on_device(): mine = lax.all_to_all(mine, 'z', 0, 0).reshape(TOK, STATE)  8.41 us
    all_to_all x1, waiting for transfers between devices, on_device(): params = jnp.sum(lax.all_to_all(params, ctx, 0, 0), axis=0)  7.62 us
    all_to_all x1, waiting for transfers between devices, on_device(): got = lax.all_to_all(scan(odd, got), ctx, 0, 0)  7.47 us
    all_to_all x1, starting transfers between devices, on_device(): got = lax.all_to_all(scan(odd, got), ctx, 0, 0)  5.55 us
  transfers between devices with their start and end apart: 6, of which 5 were waited for; matrix products, arithmetic and copies ran while one was open for 0% of the time, Pallas kernels for 6%

profile of v1, /device:TPU:8, one launch (start us, length us, event | category | flops | bytes accessed | tf_op | source)
XLA Modules:
  0.0 122.6 jit_solution(7880462731333196338)
XLA Ops:
  0.6 0.0 copy-start.11
  0.6 0.0 copy-start.12
  0.7 0.6 copy-done.11
  1.3 0.0 copy-done.12
  1.3 0.0 copy-start
  1.3 1.0 copy-done
  2.3 1.0 copy-done.2
  3.4 0.9 copy-done.4
  4.3 0.9 copy-done.6
  5.2 0.7 copy-done.8
  5.9 2.2 %states.1 = (f32[32,40,128]{2,1,0:T(8,128)}, f32[128,512]{1,0:T(8,128)S(1)}, f32[8,512]{1,0:T(8,128)S(1)}) custom-call(bf16[512,512]{1,0:T(8,128)(2,1)S(1)} %copy-done, bf16[512,512]{1,0:T(8,128)(2,1)S(1)} %copy-done.2, bf16[512,128]{1,0:T(8,128)(2,1)S(1)} %copy-done.4, bf16[512,128]{1,0:T(8,128)(2,1)S(1)} %copy-done.6, f32[8,512]{1,0:T(8,128)S(1)} %copy-done.8, ...), custom_call_target="tpu_custom_call" | custom-call | flops 2147483648 | bytes 4194304 | tf_op jit(solution)/shard_map/states/pallas_call | solution.py:320
  8.1 0.7 copy-done.21
  8.8 10.2 %all-to-all-start = ((f32[32,40,128]{2,1,0:T(8,128)}), f32[32,40,128]{2,1,0:T(8,128)S(1)}, u32[]{:S(2)}, u32[]{:S(2)}) async-start(f32[32,40,128]{2,1,0:T(8,128)} %get-tuple-element.25), calls=%async_computation | async-start | bytes 1310720 | tf_op jit(solution)/shard_map/all_to_all | solution.py:358
  19.0 19.8 %all-to-all-done.got_ref = f32[32,40,128]{2,1,0:T(8,128)S(1)} async-done(((f32[32,40,128]{2,1,0:T(8,128)}), f32[32,40,128]{2,1,0:T(8,128)S(1)}, u32[]{:S(2)}, u32[]{:S(2)}) %all-to-all-start) | async-done | bytes 655392 | tf_op jit(solution)/shard_map/all_to_all | solution.py:358
  38.8 1.0 scan.1
  39.8 5.6 %all-to-all-start.1 = ((f32[32,32,128]{2,1,0:T(8,128)}), f32[32,32,128]{2,1,0:T(8,128)S(1)}, u32[]{:S(2)}, u32[]{:S(2)}) async-start(f32[32,32,128]{2,1,0:T(8,128)} %scan.1), calls=%async_computation.1 | async-start | bytes 1048576 | tf_op jit(solution)/shard_map/all_to_all | solution.py:360
  45.4 0.0 copy-start.10
  45.4 0.0 copy-done.5
  45.4 0.0 copy-done.7
  45.4 0.0 copy-done.9
  45.4 0.0 copy-done.1
  45.5 0.0 copy-done.3
  45.5 0.6 copy-done.10
  46.1 5.0 %inner.1 = (f32[512,512]{1,0:T(8,128)S(1)}, f32[8,512]{1,0:T(8,128)S(1)}, f32[8,512]{1,0:T(8,128)S(1)}, f32[512,128]{1,0:T(8,128)S(1)}, f32[512,128]{1,0:T(8,128...) custom-call(bf16[512,512]{1,0:T(8,128)(2,1)S(1)} %copy-done.1, ...), custom_call_target="tpu_custom_call" | custom-call | flops 8589934592 | bytes 4194304 | tf_op jit(solution)/shard_map/inner/pallas_call | solution.py:336
  51.0 0.8 copy-done.13
  51.8 0.7 copy-done.15
  52.5 0.7 copy-done.17
  53.3 1.0 copy-done.19
  54.2 7.5 %all-to-all-done.1.got_ref = f32[32,32,128]{2,1,0:T(8,128)S(1)} async-done(((f32[32,32,128]{2,1,0:T(8,128)}), f32[32,32,128]{2,1,0:T(8,128)S(1)}, u32[]{:S(2)}, u32[]{:S(2)}) %all-to-all-start.1) | async-done | bytes 524320 | tf_op jit(solution)/shard_map/all_to_all | solution.py:360
  61.7 1.0 copy-done.14
  62.7 0.9 copy-done.16
  63.7 0.9 copy-done.18
  64.6 0.7 proj.1
  65.4 1.9 %collective-permute-start = (f32[512,128]{1,0:T(8,128)S(1)}, f32[512,128]{1,0:T(8,128)S(1)}, u32[]{:S(2)}, u32[]{:S(2)}) collective-permute-start(f32[512,128]{1,0:T(8,128)S(1)} %get-tuple-element.41), channel_id=1, source_target_pairs={{0,1},{1,0},{2,3},{3,2},{4,5},{5,4},{6,7},{7,6},{8,9},{9,8},{10,11... | collective-permute-start | bytes 786440 | tf_op jit(solution)/shard_map/ppermute | solution.py:363
  67.3 1.5 %collective-permute-done = f32[512,128]{1,0:T(8,128)S(1)} collective-permute-done((f32[512,128]{1,0:T(8,128)S(1)}, f32[512,128]{1,0:T(8,128)S(1)}, u32[]{:S(2)}, u32[]{:S(2)}) %collective-permute-start) | collective-permute-done | bytes 262176 | tf_op jit(solution)/shard_map/ppermute | solution.py:363
  68.9 22.4 %all_to_all.25 = f32[8,64,128]{2,1,0:T(8,128)S(1)} all-to-all(f32[8,64,128]{2,1,0:T(8,128)S(1)} %bitcast.22), channel_id=1, replica_groups=mesh['y'=8,'x'=4,'z'=8,'c'=2] {'z'}, dimensions={0} | all-to-all | bytes 524288 | tf_op jit(solution)/shard_map/all_to_all | solution.py:366
  91.3 0.7 broadcast_in_dim.2
  92.0 3.5 %all-to-all-start.3 = ((f32[8,64,128]{2,1,0:T(8,128)}), f32[8,64,128]{2,1,0:T(8,128)S(1)}, u32[]{:S(2)}, u32[]{:S(2)}) async-start(f32[8,64,128]{2,1,0:T(8,128)} %broadcast_in_dim.2), calls=%async_computation.3 | async-start | bytes 524288 | tf_op jit(solution)/shard_map/all_to_all | solution.py:368
  95.6 0.0 copy-done.20
  95.6 0.0 copy-done.22
  95.6 2.6 %close.1 = (bf16[512,512]{1,0:T(8,128)(2,1)}, f32[8,512]{1,0:T(8,128)}, f32[32,8,128]{2,1,0:T(8,128)}) custom-call(f32[32,32,128]{2,1,0:T(8,128)S(1)} %all-to-all-done.1.got_ref, bf16[512,512]{1,0:T(8,128)(2,1)S(1)} %copy-done.1, bf16[512,512]{1,0:T(8,128)(2,1)S(1)} %copy-done.3, bf16[512,128]{1,0:T(8,128)(2,1)S(1)} %copy-done.5, ...), custom_call_target="tpu_custom_call" | custom-call | flops 2147483648 | bytes 4194304 | tf_op jit(solution)/shard_map/close/pallas_call | solution.py:346
  98.2 8.4 %all-to-all-done.3 = f32[8,64,128]{2,1,0:T(8,128)S(1)} async-done(((f32[8,64,128]{2,1,0:T(8,128)}), f32[8,64,128]{2,1,0:T(8,128)S(1)}, u32[]{:S(2)}, u32[]{:S(2)}) %all-to-all-start.3) | async-done | bytes 262176 | tf_op jit(solution)/shard_map/all_to_all | solution.py:368
  106.6 5.1 %all-to-all-start.4 = ((f32[32,8,128]{2,1,0:T(8,128)}), f32[32,8,128]{2,1,0:T(8,128)S(1)}, u32[]{:S(2)}, u32[]{:S(2)}) async-start(f32[32,8,128]{2,1,0:T(8,128)} %get-tuple-element.42), calls=%async_computation.4 | async-start | bytes 262144 | tf_op jit(solution)/shard_map/all_to_all | solution.py:372
  111.7 1.9 %collective-permute-start.1 = (f32[512,128]{1,0:T(8,128)S(1)}, f32[512,128]{1,0:T(8,128)S(1)}, u32[]{:S(2)}, u32[]{:S(2)}) collective-permute-start(f32[512,128]{1,0:T(8,128)S(1)} %bitcast.23), channel_id=1, source_target_pairs={{0,1},{1,0},{2,3},{3,2},{4,5},{5,4},{6,7},{7,6},{8,9},{9,8},{10,11... | collective-permute-start | bytes 786440 | tf_op jit(solution)/shard_map/ppermute | solution.py:369
  113.6 7.6 %all-to-all-done.4 = f32[32,8,128]{2,1,0:T(8,128)S(1)} async-done(((f32[32,8,128]{2,1,0:T(8,128)}), f32[32,8,128]{2,1,0:T(8,128)S(1)}, u32[]{:S(2)}, u32[]{:S(2)}) %all-to-all-start.4) | async-done | bytes 131104 | tf_op jit(solution)/shard_map/all_to_all | solution.py:372
  121.3 0.5 slice_bitcast_fusion
  121.8 0.0 collective-permute-done.1
  121.8 0.8 broadcast_select_fusion
  (22 shorter events, 0.1 us)
Async XLA Ops:
  0.6 0.7 copy-start.11
  0.6 0.7 copy-start.12
  1.3 1.0 copy-start
  2.3 1.0 copy-start.2
  3.4 0.9 copy-start.4
  4.3 0.9 copy-start.6
  5.2 0.7 copy-start.8
  8.1 0.7 copy-start.21
  8.8 30.0 %all-to-all-start = ((f32[32,40,128]{2,1,0:T(8,128)}), f32[32,40,128]{2,1,0:T(8,128)S(1)}, u32[]{:S(2)}, u32[]{:S(2)}) async-start(f32[32,40,128]{2,1,0:T(8,128)} %get-tuple-element.25), calls=%async_computation | async-start | bytes 1310720 | tf_op jit(solution)/shard_map/all_to_all | solution.py:358
  38.8 6.6 %copy-start.5 = (bf16[512,128]{1,0:T(8,128)(2,1)S(1)}, bf16[512,128]{1,0:T(8,128)(2,1)}, u32[]{:S(2)}) copy-start(bf16[512,128]{1,0:T(8,128)(2,1)} %b_ref.5) | copy-start | bytes 393220
  38.8 6.6 %copy-start.7 = (bf16[512,128]{1,0:T(8,128)(2,1)S(1)}, bf16[512,128]{1,0:T(8,128)(2,1)}, u32[]{:S(2)}) copy-start(bf16[512,128]{1,0:T(8,128)(2,1)} %c_ref.5) | copy-start | bytes 393220
  38.8 6.6 %copy-start.9 = (f32[8,512]{1,0:T(8,128)S(1)}, f32[8,512]{1,0:T(8,128)}, u32[]{:S(2)}) copy-start(f32[8,512]{1,0:T(8,128)} %raw_ref.5) | copy-start | bytes 49156
  39.8 5.6 %copy-start.1 = (bf16[512,512]{1,0:T(8,128)(2,1)S(1)}, bf16[512,512]{1,0:T(8,128)(2,1)}, u32[]{:S(2)}) copy-start(bf16[512,512]{1,0:T(8,128)(2,1)} %x_ref.5) | copy-start | bytes 1572868
  39.8 5.6 %copy-start.3 = (bf16[512,512]{1,0:T(8,128)(2,1)S(1)}, bf16[512,512]{1,0:T(8,128)(2,1)}, u32[]{:S(2)}) copy-start(bf16[512,512]{1,0:T(8,128)(2,1)} %g_ref.5) | copy-start | bytes 1572868
  39.8 21.9 %all-to-all-start.1 = ((f32[32,32,128]{2,1,0:T(8,128)}), f32[32,32,128]{2,1,0:T(8,128)S(1)}, u32[]{:S(2)}, u32[]{:S(2)}) async-start(f32[32,32,128]{2,1,0:T(8,128)} %scan.1), calls=%async_computation.1 | async-start | bytes 1048576 | tf_op jit(solution)/shard_map/all_to_all | solution.py:360
  45.4 0.7 copy-start.10
  51.0 0.8 copy-start.13
  51.8 0.7 copy-start.15
  52.5 0.7 copy-start.17
  53.3 1.0 copy-start.19
  61.7 1.0 copy-start.14
  62.7 0.9 copy-start.16
  63.7 0.9 copy-start.18
  65.4 3.4 %collective-permute-start = (f32[512,128]{1,0:T(8,128)S(1)}, f32[512,128]{1,0:T(8,128)S(1)}, u32[]{:S(2)}, u32[]{:S(2)}) collective-permute-start(f32[512,128]{1,0:T(8,128)S(1)} %get-tuple-element.41), channel_id=1, source_target_pairs={{0,1},{1,0},{2,3},{3,2},{4,5},{5,4},{6,7},{7,6},{8,9},{9,8},{10,11... | collective-permute-start | bytes 786440 | tf_op jit(solution)/shard_map/ppermute | solution.py:363
  68.8 26.8 %copy-start.20 = (f32[512,512]{1,0:T(8,128)S(1)}, f32[512,512]{1,0:T(8,128)}, u32[]{:S(2)}) copy-start(f32[512,512]{1,0:T(8,128)} %copy-done.19) | copy-start | bytes 3145732
  92.0 3.6 %copy-start.22 = (f32[128,512]{1,0:T(8,128)S(1)}, f32[128,512]{1,0:T(8,128)}, u32[]{:S(2)}) copy-start(f32[128,512]{1,0:T(8,128)} %copy-done.21) | copy-start | bytes 786436
  92.0 14.5 %all-to-all-start.3 = ((f32[8,64,128]{2,1,0:T(8,128)}), f32[8,64,128]{2,1,0:T(8,128)S(1)}, u32[]{:S(2)}, u32[]{:S(2)}) async-start(f32[8,64,128]{2,1,0:T(8,128)} %broadcast_in_dim.2), calls=%async_computation.3 | async-start | bytes 524288 | tf_op jit(solution)/shard_map/all_to_all | solution.py:368
  106.6 14.7 %all-to-all-start.4 = ((f32[32,8,128]{2,1,0:T(8,128)}), f32[32,8,128]{2,1,0:T(8,128)S(1)}, u32[]{:S(2)}, u32[]{:S(2)}) async-start(f32[32,8,128]{2,1,0:T(8,128)} %get-tuple-element.42), calls=%async_computation.4 | async-start | bytes 262144 | tf_op jit(solution)/shard_map/all_to_all | solution.py:372
  111.7 10.1 %collective-permute-start.1 = (f32[512,128]{1,0:T(8,128)S(1)}, f32[512,128]{1,0:T(8,128)S(1)}, u32[]{:S(2)}, u32[]{:S(2)}) collective-permute-start(f32[512,128]{1,0:T(8,128)S(1)} %bitcast.23), channel_id=1, source_target_pairs={{0,1},{1,0},{2,3},{3,2},{4,5},{5,4},{6,7},{7,6},{8,9},{9,8},{10,11... | collective-permute-start | bytes 786440 | tf_op jit(solution)/shard_map/ppermute | solution.py:369

commit v2 on v1

--- a/solution.py
+++ b/solution.py
@@ -66,6 +66,17 @@
     sub = lax.broadcasted_iota(jnp.int32, (3 * HEADS, COLS), 0)
     spread = jnp.where(lane // DIM == lax.rem(sub, HEADS), 1.0, 0.0).astype(BF16)
     return mm(parts, spread)
+
+
+def expand_lanes(rows):
+    hi = rows.astype(BF16)
+    rest = rows - hi.astype(F32)
+    mid = rest.astype(BF16)
+    lo = (rest - mid.astype(F32)).astype(BF16)
+    lane = lax.broadcasted_iota(jnp.int32, (128, COLS), 1)
+    sub = lax.broadcasted_iota(jnp.int32, (128, COLS), 0)
+    spread = jnp.where(lane // DIM == sub, 1.0, 0.0).astype(BF16)
+    return mm(hi, spread) + mm(mid, spread) + mm(lo, spread)
 
 
 def softplus(v):
@@ -100,31 +111,45 @@
     return jnp.concatenate(v, axis=1), jnp.concatenate(w, axis=1) * dt
 
 
-def k_states(
-    x_ref, g_ref, b_ref, c_ref, raw_ref, rate_ref, bias_ref, send_ref, state_ref, decay_ref
-):
+def k_states(*refs):
+    sources, send_ref, local, sems = refs[:7], refs[7], refs[8:15], refs[15]
+    x_ref, g_ref, b_ref, c_ref, raw_ref, rate_ref, bias_ref = local
+    copies = [
+        pltpu.make_async_copy(source, target, sems.at[i])
+        for i, (source, target) in enumerate(zip(sources, local, strict=True))
+    ]
+    for copy in (*copies[4:], *copies[:4]):
+        copy.start()
+    for copy in copies[4:]:
+        copy.wait()
     _, dt, cum, total = decays(raw_ref, rate_ref, bias_ref)
     v, w = head_weights(dt, cum, total)
-    xw = split2(x_ref[...].astype(F32) * expand(w))
-    gv = split2(g_ref[...].astype(F32) * expand(v))
+    v, w = expand(v), expand(w)
+    copies[0].wait()
+    xw = split2(x_ref[...].astype(F32) * w)
+    copies[1].wait()
+    gv = split2(g_ref[...].astype(F32) * v)
+    copies[2].wait()
+    copies[3].wait()
     b, c = b_ref[...], c_ref[...]
     forward = mm(b, xw[0], TN) + mm(b, xw[1], TN)
     backward = mm(c, gv[0], TN) + mm(c, gv[1], TN)
-    state_ref[...] = forward
-    end = over_channels(jnp.exp2(sum(total)))
-    decay_ref[...] = jnp.broadcast_to(end, (8, COLS))
-    pieces = send_ref.shape[0]
-    for j in range(pieces):
+    end = to_row(jnp.exp2(sum(total)))
+    for j in range(send_ref.shape[0]):
         source, k = (backward if j % 2 else forward), j // 2
         for q in range(4):
-            send_ref[j, q * 8 : q * 8 + 8, :] = source[k * 8 : k * 8 + 8, q * 128 : q * 128 + 128]
-            send_ref[j, 32 + q : 33 + q, :] = end[:, q * 128 : q * 128 + 128]
-        send_ref[j, 36:40, :] = jnp.zeros((4, 128), F32)
-
-
-def k_scan(odd_ref, got_ref, out_ref):
+            tile = source[k * 8 : k * 8 + 8, q * 128 : q * 128 + 128]
+            send_ref[j, 0:1, q * 1024 : q * 1024 + 1024] = tile.reshape(1, 1024)
+        send_ref[j, 0:1, 4096:4224] = end
+
+
+def k_scan(odd_ref, got_ref, out_ref, decay_ref):
     pieces = got_ref.shape[0]
     odd = odd_ref[0]
+    ends = jnp.concatenate([got_ref[j, 0:1, 4096:4224] for j in range(pieces)], axis=0)
+    ends = expand_lanes(ends)
+    for j in range(pieces):
+        decay_ref[j] = ends[j : j + 1]
 
     def step(i, acc):
         at = jnp.where(odd == 1, pieces - 1 - i, i)
@@ -132,7 +157,8 @@
         for q in range(4):
             out_ref[at, q * 8 : q * 8 + 8, :] = acc[q]
             new.append(
-                acc[q] * got_ref[at, 32 + q : 33 + q, :] + got_ref[at, q * 8 : q * 8 + 8, :]
+                acc[q] * decay_ref[at, 0:1, q * 128 : q * 128 + 128]
+                + got_ref[at, 0:1, q * 1024 : q * 1024 + 1024].reshape(8, 128)
             )
         return tuple(new)
 
@@ -140,15 +166,16 @@
 
 
 def k_inner(
-    x_ref, g_ref, b_ref, c_ref, raw_ref, rate_ref, bias_ref, skip_ref,
+    _, x_ref, g_ref, b_ref, c_ref, raw_ref, rate_ref, bias_ref, skip_ref,
     dx_ref, rs_ref, cs_ref, db_ref, dc_ref, xh_ref, xl_ref, gh_ref, gl_ref, sk_ref,
-    score_ref, ds_ref,
+    state_ref, score_ref, ds_ref,
 ):
     _, dt, cum, total = decays(raw_ref, rate_ref, bias_ref)
     v, w = head_weights(dt, cum, total)
     x32, g32 = x_ref[...].astype(F32), g_ref[...].astype(F32)
     xh_ref[...], xl_ref[...] = split2(x32 * expand(w))
     gh_ref[...], gl_ref[...] = split2(g32 * expand(v))
+    state_ref[...] = mm(b_ref[...], xh_ref[...], TN) + mm(b_ref[...], xl_ref[...], TN)
     sk_ref[...] = jnp.broadcast_to(jnp.sum(x32 * g32, axis=0, keepdims=True), (8, COLS))
     score_ref[...] = mm(b_ref[...], c_ref[...], NT)
     rs_ref[...] = jnp.zeros_like(rs_ref)
@@ -245,10 +272,25 @@
         send_ref[...] = db
 
 
-def k_close(
+def k_fold(got_ref, out_ref):
+    total = got_ref[0]
+    for i in range(1, got_ref.shape[0]):
+        total = total + got_ref[i]
+    for i in range(out_ref.shape[0]):
+        out_ref[i] = total
+
+
+def k_dx(got_ref, part_ref, b_ref, raw_ref, rate_ref, bias_ref, dx_ref):
+    _, dt, cum, total = decays(raw_ref, rate_ref, bias_ref)
+    _, w = head_weights(dt, cum, total)
+    rh, rl = split2(join(got_ref, 1))
+    carried_u = mm(b_ref[...], rh) + mm(b_ref[...], rl)
+    dx_ref[...] = (part_ref[...] + carried_u * expand(w)).astype(BF16)
+
+
+def k_params(
     got_ref, x_ref, g_ref, b_ref, c_ref, raw_ref, rate_ref, bias_ref,
-    part_ref, rs_ref, cs_ref, state_ref, end_ref, sk_ref,
-    dx_ref, draw_ref, param_ref,
+    rs_ref, cs_ref, sk_ref, state_ref, draw_ref, param_ref,
 ):
     raw, dt, cum, total = decays(raw_ref, rate_ref, bias_ref)
     v, w = head_weights(dt, cum, total)
@@ -257,10 +299,9 @@
     rh, rl = split2(after)
     carried_y = mm(c_ref[...], sh) + mm(c_ref[...], sl)
     carried_u = mm(b_ref[...], rh) + mm(b_ref[...], rl)
-    dx_ref[...] = (part_ref[...] + carried_u * expand(w)).astype(BF16)
     rs = rs_ref[...] + v * sum_channels(g_ref[...].astype(F32) * carried_y)
     cs = cs_ref[...] + w * sum_channels(x_ref[...].astype(F32) * carried_u)
-    last = before * end_ref[0:1, :] + state_ref[...]
+    last = before * over_channels(jnp.exp2(sum(total))) + state_ref[...]
     tail = jnp.sum(after * last, axis=0, keepdims=True)
 
     def per_head(row):
@@ -289,12 +330,16 @@
     rate = to_row(-jnp.sum(da * dt, axis=1, keepdims=True))
     bias = to_row(jnp.sum(draw, axis=1, keepdims=True))
     skip = to_row(per_head(sk_ref[0:1, :]))
-    rows = jnp.concatenate([rate, bias, skip, jnp.zeros((5, 128), F32)], axis=0)
+    lane = lax.broadcasted_iota(jnp.int32, (1, 128), 1)
+    row = jnp.where(lane < HEADS, rate, 0.0)
+    row = jnp.where(lane // HEADS == 1, pltpu.roll(bias, HEADS, 1), row)
+    row = jnp.where(lane // HEADS == 2, pltpu.roll(skip, 2 * HEADS, 1), row)
     for j in range(param_ref.shape[0]):
-        param_ref[j] = rows
+        param_ref[j] = row
 
 
 VMEM = pl.BlockSpec(memory_space=pltpu.VMEM)
+HBM = pl.BlockSpec(memory_space=pltpu.HBM)
 SMEM = pl.BlockSpec(memory_space=pltpu.SMEM)
 
 
@@ -302,48 +347,82 @@
     return jax.ShapeDtypeStruct(dims, dtype)
 
 
-def call(body, name, specs, outs, flops, scratch=()):
+def fetched(body, count, first, *refs):
+    local, sems = refs[-1 - (count - first) : -1], refs[-1]
+    copies = [
+        pltpu.make_async_copy(source, target, sems.at[i])
+        for i, (source, target) in enumerate(zip(refs[first:count], local, strict=True))
+    ]
+    for copy in copies:
+        copy.start()
+    for copy in copies:
+        copy.wait()
+    body(*refs[:first], *local, *refs[count : -1 - (count - first)])
+
+
+def call(body, name, args, outs, flops, first=None, scratch=(), specs=()):
+    count, scratch = len(args), list(scratch)
+    first = count if first is None else first
+    if first < count:
+        scratch += [pltpu.VMEM(a.shape, a.dtype) for a in args[first:]]
+        scratch.append(pltpu.SemaphoreType.DMA((count - first,)))
+        args = [
+            *args[:first],
+            *(pltpu.with_memory_space_constraint(a, pltpu.HBM) for a in args[first:]),
+        ]
+        if first:
+            body = functools.partial(fetched, body, count, first)
+    specs = list(specs) + [VMEM] * (first - len(specs)) + [HBM] * (count - first)
     return pl.pallas_call(
         body,
         in_specs=specs,
         out_specs=[VMEM] * len(outs),
         out_shape=outs,
-        scratch_shapes=list(scratch),
-        compiler_params=pltpu.CompilerParams(vmem_limit_bytes=48 << 20),
+        scratch_shapes=scratch,
+        compiler_params=pltpu.CompilerParams(vmem_limit_bytes=24 << 20),
         cost_estimate=pl.CostEstimate(flops=flops, bytes_accessed=4 << 20, transcendentals=0),
         name=name,
-    )
+    )(*args)
 
 
 def states(pieces, *args):
-    outs = [shape((pieces, 40, 128)), shape((STATE, COLS)), shape((8, COLS))]
-    return call(k_states, "states", [VMEM] * 7, outs, 1 << 31)(*args)
+    return call(k_states, "states", args, [shape((pieces, 1, 4224))], 1 << 31, 0)[0]
 
 
 def scan(odd, got):
     out = [shape((got.shape[0], 32, 128))]
-    return call(k_scan, "scan", [SMEM, VMEM], out, 1 << 28)(odd, got)[0]
-
-
-def inner(*args):
+    scratch = [pltpu.VMEM((got.shape[0], 1, COLS), F32)]
+    return call(k_scan, "scan", (odd, got), out, 1 << 28, scratch=scratch, specs=[SMEM])[0]
+
+
+def inner(odd, *args):
     outs = [
         shape((TOK, COLS)), shape((HEADS, TOK)), shape((HEADS, TOK)),
         shape((TOK, STATE)), shape((TOK, STATE)),
         shape((TOK, COLS), BF16), shape((TOK, COLS), BF16),
-        shape((TOK, COLS), BF16), shape((TOK, COLS), BF16), shape((8, COLS)),
+        shape((TOK, COLS), BF16), shape((TOK, COLS), BF16),
+        shape((8, COLS)), shape((STATE, COLS)),
     ]
     scratch = [pltpu.VMEM((TOK, TOK), F32), pltpu.VMEM((TOK, TOK), F32)]
-    return call(k_inner, "inner", [VMEM] * 8, outs, 1 << 33, scratch)(*args)
+    return call(k_inner, "inner", (odd, *args), outs, 1 << 33, 1, scratch, [SMEM])
 
 
 def proj(*args):
     outs = [shape((TOK, STATE)), shape((TOK, STATE))]
-    return call(k_proj, "proj", [SMEM] + [VMEM] * 7, outs, 1 << 30)(*args)
-
-
-def close(pieces, *args):
-    outs = [shape((TOK, COLS), BF16), shape((HEADS, TOK)), shape((pieces, 8, 128))]
-    return call(k_close, "close", [VMEM] * 14, outs, 1 << 31)(*args)
+    return call(k_proj, "proj", args, outs, 1 << 30, specs=[SMEM])
+
+
+def params(pieces, *args):
+    outs = [shape((HEADS, TOK)), shape((pieces, 1, 128))]
+    return call(k_params, "params", args, outs, 1 << 30, 1)
+
+
+def dx(*args):
+    return call(k_dx, "dx", args, [shape((TOK, COLS), BF16)], 1 << 30, 1)[0]
+
+
+def fold(got):
+    return call(k_fold, "fold", (got,), [shape(got.shape)], 1 << 20)[0]
 
 
 def on_device(tokens_x, raw_dt, in_b, in_c, decay_rate, skip_gain, step_bias, grad_y):
@@ -354,25 +433,25 @@
     rate, skip, bias = (a.reshape(1, HEADS) for a in (decay_rate, skip_gain, step_bias))
     data = (tokens_x, grad_y, in_b, in_c, raw_dt, rate, bias)
 
-    send, state, end = states(pieces, *data)
+    send = states(pieces, *data)
     got = lax.all_to_all(send, ctx, 0, 0)
-    part, rs, cs, db, dc, xh, xl, gh, gl, sk = inner(*data, skip)
+    part, rs, cs, db, dc, xh, xl, gh, gl, sk, state = inner(odd, *data, skip)
     got = lax.all_to_all(scan(odd, got), ctx, 0, 0)
     keep, send = proj(core, got, xh, xl, gh, gl, db, dc)
     swap = [(0, 1), (1, 0)]
     mine = keep + lax.ppermute(send, "c", swap)
-    grad_x, grad_raw, params = close(pieces, got, *data, part, rs, cs, state, end, sk)
+    grad_raw, partial = params(pieces, got, *data, rs, cs, sk, state)
     ranks = lax.axis_size("z")
     mine = lax.all_to_all(mine.reshape(ranks, TOK // ranks, STATE), "z", 0, 0)
-    mine = jnp.broadcast_to(jnp.sum(mine, axis=0)[None], mine.shape)
-    mine = lax.all_to_all(mine, "z", 0, 0).reshape(TOK, STATE)
+    grad_x = dx(got, part, in_b, raw_dt, rate, bias)
+    mine = lax.all_to_all(fold(mine), "z", 0, 0).reshape(TOK, STATE)
     other = lax.ppermute(mine, "c", swap)
+    partial = jnp.sum(lax.all_to_all(partial, ctx, 0, 0), axis=(0, 1))
     first = core[0] == 0
     grad_b, grad_c = jnp.where(first, mine, other), jnp.where(first, other, mine)
-    params = jnp.sum(lax.all_to_all(params, ctx, 0, 0), axis=0)
     return (
         grad_x, grad_raw, grad_b, grad_c,
-        params[0, :HEADS], params[2, :HEADS], params[1, :HEADS],
+        partial[:HEADS], partial[2 * HEADS : 3 * HEADS], partial[HEADS : 2 * HEADS],
     )
 
 

time: 124 us -> 112 us (0.903)
  the two profiles are of different devices: /device:TPU:8 before, /device:TPU:2 now
where the time goes in v2:
time: 112 us
  waiting for transfers between devices  35.5 us (32%)
  starting transfers between devices  28.6 us (26%)
  blocking collectives  22.3 us (20%)
  Pallas kernels  19.5 us (17%)
  local copies, waits for them, and re-layouts  4.07 us (4%)
    all_to_all x1, blocking collectives, on_device(): mine = lax.all_to_all(mine.reshape(ranks, TOK // ranks, STATE), 'z', 0, 0)  22.3 us
    pallas_call x7, Pallas kernels, call(): pl.pallas_call(body, in_specs=specs, out_specs=[VMEM] * len(outs), out_sh...  19.5 us
    all_to_all x1, waiting for transfers between devices, on_device(): got = lax.all_to_all(send, ctx, 0, 0)  17.2 us
    all_to_all x1, starting transfers between devices, on_device(): got = lax.all_to_all(send, ctx, 0, 0)  10.3 us
    all_to_all x1, waiting for transfers between devices, on_device(): mine = lax.all_to_all(fold(mine), 'z', 0, 0).reshape(TOK, STATE)  7.06 us
    all_to_all x1, waiting for transfers between devices, on_device(): got = lax.all_to_all(scan(odd, got), ctx, 0, 0)  6.01 us
    all_to_all x1, starting transfers between devices, on_device(): partial = jnp.sum(lax.all_to_all(partial, ctx, 0, 0), axis=(0, 1))  5.57 us
    all_to_all x1, starting transfers between devices, on_device(): got = lax.all_to_all(scan(odd, got), ctx, 0, 0)  5.57 us
  transfers between devices with their start and end apart: 6, of which 5 were waited for; matrix products, arithmetic and copies ran while one was open for 1% of the time, Pallas kernels for 12%

profile of v2, /device:TPU:2, one launch (start us, length us, event | category | flops | bytes accessed | tf_op | source)
XLA Modules:
  0.0 111.7 jit_solution(8064447266205788951)
XLA Ops:
  0.6 3.7 %states.1 = f32[32,1,4224]{2,1,0:T(1,128)} custom-call(bf16[512,512]{1,0:T(8,128)(2,1)} %refs_1_.5, bf16[512,512]{1,0:T(8,128)(2,1)} %refs_2_.7, bf16[512,128]{1,0:T(8,128)(2,1)} %refs_3_.7, bf16[512,128]{1,0:T(8,128)(2,1)} %refs_4_.5, f32[8,512]{1,0:T(8,128)} %refs_5_.3, f32[1,8]{1,0:T(1,128)} %bitcast.12, f32[1,8]{1,0:T(1,128)} %bitcast.16), custom_call_target="tpu_custom_call" | custom-call | flops 2147483648 | bytes 4194304 | tf_op jit(solution)/shard_map/states/pallas_call | solution.py:376
  4.3 10.3 %all-to-all-start = ((f32[32,1,4224]{2,1,0:T(1,128)}), f32[32,1,4224]{2,1,0:T(1,128)S(1)}, u32[]{:S(2)}, u32[]{:S(2)}) async-start(f32[32,1,4224]{2,1,0:T(1,128)} %states.1), calls=%async_computation | async-start | bytes 1081344 | tf_op jit(solution)/shard_map/all_to_all | solution.py:437
  14.6 17.2 %all-to-all-done.got_ref = f32[32,1,4224]{2,1,0:T(1,128)S(1)} async-done(((f32[32,1,4224]{2,1,0:T(1,128)}), f32[32,1,4224]{2,1,0:T(1,128)S(1)}, u32[]{:S(2)}, u32[]{:S(2)}) %all-to-all-start) | async-done | bytes 540704 | tf_op jit(solution)/shard_map/all_to_all | solution.py:437
  31.8 1.2 %scan.1 = f32[32,32,128]{2,1,0:T(8,128)} custom-call(s32[1]{0:T(128)} %bitcast.odd_ref.refs_0_, f32[32,1,4224]{2,1,0:T(1,128)S(1)} %all-to-all-done.got_ref), custom_call_target="tpu_custom_call" | custom-call | flops 268435456 | bytes 4194304 | tf_op jit(solution)/shard_map/scan/pallas_call | solution.py:376
  33.0 5.6 %all-to-all-start.1 = ((f32[32,32,128]{2,1,0:T(8,128)}), f32[32,32,128]{2,1,0:T(8,128)S(1)}, u32[]{:S(2)}, u32[]{:S(2)}) async-start(f32[32,32,128]{2,1,0:T(8,128)} %scan.1), calls=%async_computation.1 | async-start | bytes 1048576 | tf_op jit(solution)/shard_map/all_to_all | solution.py:439
  38.5 6.4 %inner.1 = (f32[512,512]{1,0:T(8,128)S(1)}, f32[8,512]{1,0:T(8,128)S(1)}, f32[8,512]{1,0:T(8,128)S(1)}, f32[512,128]{1,0:T(8,128)S(1)}, f32[512,128]{1,0:T(8,128...) custom-call(s32[1]{0:T(128)} %bitcast.odd_ref.refs_0_, ...), custom_call_target="tpu_custom_call" | custom-call | flops 8589934592 | bytes 4194304 | tf_op jit(solution)/shard_map/inner/pallas_call | solution.py:376
  45.0 0.0 copy-start
  45.0 1.0 copy-done
  46.0 0.0 copy-start.1
  46.0 0.7 copy-done.1
  46.7 0.0 copy-start.2
  46.7 0.6 copy-done.2
  47.3 0.0 copy-start.3
  47.3 0.6 copy-done.3
  47.9 0.0 copy-start.4
  47.9 0.6 copy-done.4
  48.5 6.0 %all-to-all-done.1.refs_0_.got_ref = f32[32,32,128]{2,1,0:T(8,128)S(1)} async-done(((f32[32,32,128]{2,1,0:T(8,128)}), f32[32,32,128]{2,1,0:T(8,128)S(1)}, u32[]{:S(2)}, u32[]{:S(2)}) %all-to-all-start.1) | async-done | bytes 524320 | tf_op jit(solution)/shard_map/all_to_all | solution.py:439
  54.5 0.7 proj.1
  55.2 1.9 %collective-permute-start = (f32[512,128]{1,0:T(8,128)S(1)}, f32[512,128]{1,0:T(8,128)S(1)}, u32[]{:S(2)}, u32[]{:S(2)}) collective-permute-start(f32[512,128]{1,0:T(8,128)S(1)} %get-tuple-element.35), channel_id=1, source_target_pairs={{0,1},{1,0},{2,3},{3,2},{4,5},{5,4},{6,7},{7,6},{8,9},{9,8},{10,11... | collective-permute-start | bytes 786440 | tf_op jit(solution)/shard_map/ppermute | solution.py:442
  57.2 1.5 %collective-permute-done = f32[512,128]{1,0:T(8,128)S(1)} collective-permute-done((f32[512,128]{1,0:T(8,128)S(1)}, f32[512,128]{1,0:T(8,128)S(1)}, u32[]{:S(2)}, u32[]{:S(2)}) %collective-permute-start) | collective-permute-done | bytes 262176 | tf_op jit(solution)/shard_map/ppermute | solution.py:442
  58.7 22.3 %all_to_all.25.got_ref = f32[8,64,128]{2,1,0:T(8,128)S(1)} all-to-all(f32[8,64,128]{2,1,0:T(8,128)S(1)} %bitcast.9), channel_id=1, replica_groups=mesh['y'=8,'x'=4,'z'=8,'c'=2] {'z'}, dimensions={0} | all-to-all | bytes 524288 | tf_op jit(solution)/shard_map/all_to_all | solution.py:445
  81.0 0.7 fold.1
  81.7 3.4 %all-to-all-start.3 = ((f32[8,64,128]{2,1,0:T(8,128)}), f32[8,64,128]{2,1,0:T(8,128)S(1)}, u32[]{:S(2)}, u32[]{:S(2)}) async-start(f32[8,64,128]{2,1,0:T(8,128)} %fold.1), calls=%async_computation.3 | async-start | bytes 524288 | tf_op jit(solution)/shard_map/all_to_all | solution.py:447
  85.1 3.9 %params.1 = (f32[8,512]{1,0:T(8,128)}, f32[32,1,128]{2,1,0:T(1,128)}) custom-call(f32[32,32,128]{2,1,0:T(8,128)S(1)} %all-to-all-done.1.refs_0_.got_ref, bf16[512,512]{1,0:T(8,128)(2,1)} %refs_1_.5, bf16[512,512]{1,0:T(8,128)(2,1)} %refs_2_.7, bf16[512,128]{1,0:T(8,128)(2,1)} %refs_3_.7, bf16[512,128]{1,0:T(8,128)(2,1)} %refs_4_.5, f32[8,512]{1,0:T(8,128)} %refs_5_.3, ...), custom_call_target="tpu_custom_call" | custom-call | flops 1073741824 | bytes 4194304 | tf_op jit(solution)/shard_map/params/pallas_call | solution.py:376
  89.1 7.1 %all-to-all-done.3 = f32[8,64,128]{2,1,0:T(8,128)S(1)} async-done(((f32[8,64,128]{2,1,0:T(8,128)}), f32[8,64,128]{2,1,0:T(8,128)S(1)}, u32[]{:S(2)}, u32[]{:S(2)}) %all-to-all-start.3) | async-done | bytes 262176 | tf_op jit(solution)/shard_map/all_to_all | solution.py:447
  96.1 5.6 %all-to-all-start.4 = ((f32[32,1,128]{2,1,0:T(1,128)}), f32[32,1,128]{2,1,0:T(1,128)S(1)}, u32[]{:S(2)}, u32[]{:S(2)}) async-start(f32[32,1,128]{2,1,0:T(1,128)} %get-tuple-element.36), calls=%async_computation.4 | async-start | bytes 32768 | tf_op jit(solution)/shard_map/all_to_all | solution.py:449
  101.7 1.9 %collective-permute-start.1 = (f32[512,128]{1,0:T(8,128)S(1)}, f32[512,128]{1,0:T(8,128)S(1)}, u32[]{:S(2)}, u32[]{:S(2)}) collective-permute-start(f32[512,128]{1,0:T(8,128)S(1)} %bitcast.10), channel_id=1, source_target_pairs={{0,1},{1,0},{2,3},{3,2},{4,5},{5,4},{6,7},{7,6},{8,9},{9,8},{10,11... | collective-permute-start | bytes 786440 | tf_op jit(solution)/shard_map/ppermute | solution.py:448
  103.6 2.9 %dx.1 = bf16[512,512]{1,0:T(8,128)(2,1)} custom-call(f32[32,32,128]{2,1,0:T(8,128)S(1)} %all-to-all-done.1.refs_0_.got_ref, f32[512,512]{1,0:T(8,128)} %copy-done, bf16[512,128]{1,0:T(8,128)(2,1)} %refs_3_.7, f32[8,512]{1,0:T(8,128)} %refs_5_.3, f32[1,8]{1,0:T(1,128)} %bitcast.15, f32[1,8]{1,0:T(1,128)} %bitcast.19), custom_call_target="tpu_custom_call" | custom-call | flops 1073741824 | bytes 4194304 | tf_op jit(solution)/shard_map/dx/pallas_call | solution.py:376
  106.5 3.7 %all-to-all-done.4 = f32[32,1,128]{2,1,0:T(1,128)S(1)} async-done(((f32[32,1,128]{2,1,0:T(1,128)}), f32[32,1,128]{2,1,0:T(1,128)S(1)}, u32[]{:S(2)}, u32[]{:S(2)}) %all-to-all-start.4) | async-done | bytes 16416 | tf_op jit(solution)/shard_map/all_to_all | solution.py:449
  110.2 0.1 reduce_sum.9
  110.3 0.6 fusion
  110.9 0.0 collective-permute-done.1
  110.9 0.8 broadcast_select_fusion
  (1 shorter events, 0.0 us)
Async XLA Ops:
  4.3 27.5 %all-to-all-start = ((f32[32,1,4224]{2,1,0:T(1,128)}), f32[32,1,4224]{2,1,0:T(1,128)S(1)}, u32[]{:S(2)}, u32[]{:S(2)}) async-start(f32[32,1,4224]{2,1,0:T(1,128)} %states.1), calls=%async_computation | async-start | bytes 1081344 | tf_op jit(solution)/shard_map/all_to_all | solution.py:437
  33.0 21.5 %all-to-all-start.1 = ((f32[32,32,128]{2,1,0:T(8,128)}), f32[32,32,128]{2,1,0:T(8,128)S(1)}, u32[]{:S(2)}, u32[]{:S(2)}) async-start(f32[32,32,128]{2,1,0:T(8,128)} %scan.1), calls=%async_computation.1 | async-start | bytes 1048576 | tf_op jit(solution)/shard_map/all_to_all | solution.py:439
  45.0 1.0 copy-start
  46.0 0.7 copy-start.1
  46.7 0.6 copy-start.2
  47.3 0.6 copy-start.3
  47.9 0.6 copy-start.4
  55.2 3.4 %collective-permute-start = (f32[512,128]{1,0:T(8,128)S(1)}, f32[512,128]{1,0:T(8,128)S(1)}, u32[]{:S(2)}, u32[]{:S(2)}) collective-permute-start(f32[512,128]{1,0:T(8,128)S(1)} %get-tuple-element.35), channel_id=1, source_target_pairs={{0,1},{1,0},{2,3},{3,2},{4,5},{5,4},{6,7},{7,6},{8,9},{9,8},{10,11... | collective-permute-start | bytes 786440 | tf_op jit(solution)/shard_map/ppermute | solution.py:442
  81.7 14.4 %all-to-all-start.3 = ((f32[8,64,128]{2,1,0:T(8,128)}), f32[8,64,128]{2,1,0:T(8,128)S(1)}, u32[]{:S(2)}, u32[]{:S(2)}) async-start(f32[8,64,128]{2,1,0:T(8,128)} %fold.1), calls=%async_computation.3 | async-start | bytes 524288 | tf_op jit(solution)/shard_map/all_to_all | solution.py:447
  96.1 14.1 %all-to-all-start.4 = ((f32[32,1,128]{2,1,0:T(1,128)}), f32[32,1,128]{2,1,0:T(1,128)S(1)}, u32[]{:S(2)}, u32[]{:S(2)}) async-start(f32[32,1,128]{2,1,0:T(1,128)} %get-tuple-element.36), calls=%async_computation.4 | async-start | bytes 32768 | tf_op jit(solution)/shard_map/all_to_all | solution.py:449
  101.7 9.2 %collective-permute-start.1 = (f32[512,128]{1,0:T(8,128)S(1)}, f32[512,128]{1,0:T(8,128)S(1)}, u32[]{:S(2)}, u32[]{:S(2)}) collective-permute-start(f32[512,128]{1,0:T(8,128)S(1)} %bitcast.10), channel_id=1, source_target_pairs={{0,1},{1,0},{2,3},{3,2},{4,5},{5,4},{6,7},{7,6},{8,9},{9,8},{10,11... | collective-permute-start | bytes 786440 | tf_op jit(solution)/shard_map/ppermute | solution.py:448

commit v3 on v2

--- a/solution.py
+++ b/solution.py
@@ -47,6 +47,21 @@
     return lane // DIM == sub
 
 
+def block_sums(rows, reverse):
+    stacked = jnp.concatenate([rows[:, b * TB : (b + 1) * TB] for b in range(NB)], axis=0)
+    hi = stacked.astype(BF16)
+    rest = stacked - hi.astype(F32)
+    mid = rest.astype(BF16)
+    lo = (rest - mid.astype(F32)).astype(BF16)
+    s = lax.broadcasted_iota(jnp.int32, (TB, TB), 0)
+    t = lax.broadcasted_iota(jnp.int32, (TB, TB), 1)
+    ones = jnp.where(s >= t if reverse else s <= t, 1.0, 0.0).astype(BF16)
+    sums = mm(jnp.concatenate([hi, mid, lo], axis=0), ones)
+    n = NB * HEADS
+    sums = sums[:n] + (sums[n : 2 * n] + sums[2 * n :])
+    return [sums[b * HEADS : (b + 1) * HEADS] for b in range(NB)]
+
+
 def over_channels(column):
     return jnp.sum(jnp.where(member(), column, 0.0), axis=0, keepdims=True)
 
@@ -90,14 +105,7 @@
     raw = raw_ref[...] + to_column(bias_ref[...])
     dt = softplus(raw)
     a = -(to_column(rate_ref[...]) * LOG2E) * dt
-    stacked = jnp.concatenate([a[:, b * TB : (b + 1) * TB] for b in range(NB)], axis=0)
-    s = lax.broadcasted_iota(jnp.int32, (TB, TB), 0)
-    t = lax.broadcasted_iota(jnp.int32, (TB, TB), 1)
-    upto = jnp.where(s <= t, 1.0, 0.0)
-    cum = lax.dot_general(
-        stacked, upto, NN, precision=lax.Precision.HIGHEST, preferred_element_type=F32
-    )
-    cum = [cum[b * HEADS : (b + 1) * HEADS] for b in range(NB)]
+    cum = block_sums(a, False)
     total = [c[:, TB - 1 : TB] for c in cum]
     return raw, dt, cum, total
 
@@ -155,14 +163,15 @@
         at = jnp.where(odd == 1, pieces - 1 - i, i)
         new = []
         for q in range(4):
-            out_ref[at, q * 8 : q * 8 + 8, :] = acc[q]
+            out_ref[at, 0:1, q * 1024 : q * 1024 + 1024] = acc[q].reshape(1, 1024)
             new.append(
                 acc[q] * decay_ref[at, 0:1, q * 128 : q * 128 + 128]
                 + got_ref[at, 0:1, q * 1024 : q * 1024 + 1024].reshape(8, 128)
             )
         return tuple(new)
 
-    lax.fori_loop(0, pieces, step, tuple(jnp.zeros((8, 128), F32) for _ in range(4)))
+    zero = tuple(jnp.zeros((8, 128), F32) for _ in range(4))
+    lax.fori_loop(0, pieces, step, zero, unroll=8)
 
 
 def k_inner(
@@ -243,7 +252,11 @@
     return jnp.concatenate(
         [
             jnp.concatenate(
-                [got_ref[2 * k + odd, q * 8 : q * 8 + 8, :] for q in range(4)], axis=1
+                [
+                    got_ref[2 * k + odd, 0:1, q * 1024 : q * 1024 + 1024].reshape(8, 128)
+                    for q in range(4)
+                ],
+                axis=1,
             )
             for k in range(got_ref.shape[0] // 2)
         ],
@@ -307,21 +320,11 @@
     def per_head(row):
         return jnp.sum(jnp.where(member(), row, 0.0), axis=1, keepdims=True)
 
-    dcum = rs - cs
-    stacked = jnp.concatenate([dcum[:, b * TB : (b + 1) * TB] for b in range(NB)], axis=0)
-    s = lax.broadcasted_iota(jnp.int32, (TB, TB), 0)
-    t = lax.broadcasted_iota(jnp.int32, (TB, TB), 1)
-    down = lax.dot_general(
-        stacked,
-        jnp.where(s >= t, 1.0, 0.0),
-        NN,
-        precision=lax.Precision.HIGHEST,
-        preferred_element_type=F32,
-    )
+    down = block_sums(rs - cs, True)
     later = per_head(tail)
     da = [None] * NB
     for b in reversed(range(NB)):
-        here = down[b * HEADS : (b + 1) * HEADS]
+        here = down[b]
         da[b] = here + later
         later = later + here[:, 0:1]
     da = jnp.concatenate(da, axis=1)
@@ -390,7 +393,7 @@
 
 
 def scan(odd, got):
-    out = [shape((got.shape[0], 32, 128))]
+    out = [shape((got.shape[0], 1, 4096))]
     scratch = [pltpu.VMEM((got.shape[0], 1, COLS), F32)]
     return call(k_scan, "scan", (odd, got), out, 1 << 28, scratch=scratch, specs=[SMEM])[0]
 
@@ -434,6 +437,7 @@
     data = (tokens_x, grad_y, in_b, in_c, raw_dt, rate, bias)
 
     send = states(pieces, *data)
+    send, odd, core = lax.optimization_barrier((send, odd, core))
     got = lax.all_to_all(send, ctx, 0, 0)
     part, rs, cs, db, dc, xh, xl, gh, gl, sk, state = inner(odd, *data, skip)
     got = lax.all_to_all(scan(odd, got), ctx, 0, 0)

time: 112 us -> 111 us (level)
  blocking collectives: 22.3 us -> 49.5 us
  waiting for transfers between devices: 35.5 us -> 18.5 us
  starting transfers between devices: 28.6 us -> 18.4 us
  Pallas kernels: 19.5 us -> 18.2 us
    all_to_all x0 -> x1, blocking collectives: none -> 27.2 us  [on_device(): got = lax.all_to_all(send, ctx, 0, 0)]
    all_to_all x1 -> x0, waiting for transfers between devices: 17.2 us -> none  [on_device(): got = lax.all_to_all(send, ctx, 0, 0)]
    all_to_all x1 -> x0, starting transfers between devices: 10.3 us -> none  [on_device(): got = lax.all_to_all(send, ctx, 0, 0)]
    pallas_call x7, Pallas kernels: 19.5 us -> 18.2 us  [call(): pl.pallas_call(body, in_specs=specs, out_specs=[VMEM] * len(outs), out_sh...]
  transfers between devices with their start and end apart: 6 -> 5, of which waited for: 5 -> 4; matrix products, arithmetic and copies ran while one was open for 1% -> 1% of each run, Pallas kernels for 12% -> 12%
where the time goes in v3:
time: 111 us; the launch traced here: 110 us
  blocking collectives  49.5 us (45%)
  waiting for transfers between devices  18.5 us (17%)
  starting transfers between devices  18.4 us (17%)
  Pallas kernels  18.2 us (16%)
  local copies, waits for them, and re-layouts  4.06 us (4%)
    all_to_all x1, blocking collectives, on_device(): got = lax.all_to_all(send, ctx, 0, 0)  27.2 us
    all_to_all x1, blocking collectives, on_device(): mine = lax.all_to_all(mine.reshape(ranks, TOK // ranks, STATE), 'z', 0, 0)  22.3 us
    pallas_call x7, Pallas kernels, call(): pl.pallas_call(body, in_specs=specs, out_specs=[VMEM] * len(outs), out_sh...  18.2 us
    all_to_all x1, waiting for transfers between devices, on_device(): mine = lax.all_to_all(fold(mine), 'z', 0, 0).reshape(TOK, STATE)  7.22 us
    all_to_all x1, waiting for transfers between devices, on_device(): got = lax.all_to_all(scan(odd, got), ctx, 0, 0)  5.96 us
    all_to_all x1, starting transfers between devices, on_device(): got = lax.all_to_all(scan(odd, got), ctx, 0, 0)  5.57 us
    all_to_all x1, starting transfers between devices, on_device(): partial = jnp.sum(lax.all_to_all(partial, ctx, 0, 0), axis=(0, 1))  5.56 us
    all_to_all x1, waiting for transfers between devices, on_device(): partial = jnp.sum(lax.all_to_all(partial, ctx, 0, 0), axis=(0, 1))  3.84 us
  transfers between devices with their start and end apart: 5, of which 4 were waited for; matrix products, arithmetic and copies ran while one was open for 1% of the time, Pallas kernels for 12%

profile of v3, /device:TPU:2, one launch (start us, length us, event | category | flops | bytes accessed | tf_op | source)
XLA Modules:
  0.0 110.4 jit_solution(18438879974942479145)
XLA Ops:
  0.6 2.7 %states.1 = f32[32,1,4224]{2,1,0:T(1,128)S(1)} custom-call(bf16[512,512]{1,0:T(8,128)(2,1)} %refs_1_.5, bf16[512,512]{1,0:T(8,128)(2,1)} %refs_2_.7, bf16[512,128]{1,0:T(8,128)(2,1)} %refs_3_.7, bf16[512,128]{1,0:T(8,128)(2,1)} %refs_4_.5, f32[8,512]{1,0:T(8,128)} %refs_5_.3, f32[1,8]{1,0:T(1,128)} %bitcast.13, f32[1,8]{1,0:T(1,128)} %bitcast.17), custom_call_target="tpu_custom_call" | custom-call | flops 2147483648 | bytes 4194304 | tf_op jit(solution)/shard_map/states/pallas_call | solution.py:379
  3.3 27.2 %all_to_all.25.got_ref = f32[32,1,4224]{2,1,0:T(1,128)S(1)} all-to-all(f32[32,1,4224]{2,1,0:T(1,128)S(1)} %states.1), channel_id=1, replica_groups=mesh['y'=8,'x'=4,'z'=8,'c'=2] {'y','x'}, dimensions={0} | all-to-all | bytes 1081344 | tf_op jit(solution)/shard_map/all_to_all | solution.py:441
  30.6 1.1 scan.1
  31.7 5.6 %all-to-all-start.1 = ((f32[32,1,4096]{2,1,0:T(1,128)}), f32[32,1,4096]{2,1,0:T(1,128)S(1)}, u32[]{:S(2)}, u32[]{:S(2)}) async-start(f32[32,1,4096]{2,1,0:T(1,128)} %scan.1), calls=%async_computation.1 | async-start | bytes 1048576 | tf_op jit(solution)/shard_map/all_to_all | solution.py:443
  37.2 6.5 %inner.1 = (f32[512,512]{1,0:T(8,128)S(1)}, f32[8,512]{1,0:T(8,128)S(1)}, f32[8,512]{1,0:T(8,128)S(1)}, f32[512,128]{1,0:T(8,128)S(1)}, f32[512,128]{1,0:T(8,128...) custom-call(s32[1]{0:T(128)} %bitcast.2.odd_ref.refs_0_, ...), custom_call_target="tpu_custom_call" | custom-call | flops 8589934592 | bytes 4194304 | tf_op jit(solution)/shard_map/inner/pallas_call | solution.py:379
  43.7 0.0 copy-start
  43.7 1.0 copy-done
  44.7 0.0 copy-start.1
  44.7 0.7 copy-done.1
  45.4 0.0 copy-start.2
  45.4 0.6 copy-done.2
  46.0 0.0 copy-start.3
  46.0 0.6 copy-done.3
  46.6 0.0 copy-start.4
  46.6 0.6 copy-done.4
  47.2 6.0 %all-to-all-done.1.refs_0_.got_ref = f32[32,1,4096]{2,1,0:T(1,128)S(1)} async-done(((f32[32,1,4096]{2,1,0:T(1,128)}), f32[32,1,4096]{2,1,0:T(1,128)S(1)}, u32[]{:S(2)}, u32[]{:S(2)}) %all-to-all-start.1) | async-done | bytes 524320 | tf_op jit(solution)/shard_map/all_to_all | solution.py:443
  53.2 0.7 proj.1
  53.9 1.9 %collective-permute-start = (f32[512,128]{1,0:T(8,128)S(1)}, f32[512,128]{1,0:T(8,128)S(1)}, u32[]{:S(2)}, u32[]{:S(2)}) collective-permute-start(f32[512,128]{1,0:T(8,128)S(1)} %get-tuple-element.41), channel_id=1, source_target_pairs={{0,1},{1,0},{2,3},{3,2},{4,5},{5,4},{6,7},{7,6},{8,9},{9,8},{10,11... | collective-permute-start | bytes 786440 | tf_op jit(solution)/shard_map/ppermute | solution.py:446
  55.8 1.5 %collective-permute-done = f32[512,128]{1,0:T(8,128)S(1)} collective-permute-done((f32[512,128]{1,0:T(8,128)S(1)}, f32[512,128]{1,0:T(8,128)S(1)}, u32[]{:S(2)}, u32[]{:S(2)}) %collective-permute-start) | collective-permute-done | bytes 262176 | tf_op jit(solution)/shard_map/ppermute | solution.py:446
  57.4 22.3 %all_to_all.26.got_ref = f32[8,64,128]{2,1,0:T(8,128)S(1)} all-to-all(f32[8,64,128]{2,1,0:T(8,128)S(1)} %bitcast.10), channel_id=1, replica_groups=mesh['y'=8,'x'=4,'z'=8,'c'=2] {'z'}, dimensions={0} | all-to-all | bytes 524288 | tf_op jit(solution)/shard_map/all_to_all | solution.py:449
  79.7 0.7 fold.1
  80.4 3.4 %all-to-all-start.3 = ((f32[8,64,128]{2,1,0:T(8,128)}), f32[8,64,128]{2,1,0:T(8,128)S(1)}, u32[]{:S(2)}, u32[]{:S(2)}) async-start(f32[8,64,128]{2,1,0:T(8,128)} %fold.1), calls=%async_computation.3 | async-start | bytes 524288 | tf_op jit(solution)/shard_map/all_to_all | solution.py:451
  83.8 3.8 %params.1 = (f32[8,512]{1,0:T(8,128)}, f32[32,1,128]{2,1,0:T(1,128)}) custom-call(f32[32,1,4096]{2,1,0:T(1,128)S(1)} %all-to-all-done.1.refs_0_.got_ref, bf16[512,512]{1,0:T(8,128)(2,1)} %refs_1_.5, bf16[512,512]{1,0:T(8,128)(2,1)} %refs_2_.7, bf16[512,128]{1,0:T(8,128)(2,1)} %refs_3_.7, bf16[512,128]{1,0:T(8,128)(2,1)} %refs_4_.5, f32[8,512]{1,0:T(8,128)} %refs_5_.3, ...), custom_call_target="tpu_custom_call" | custom-call | flops 1073741824 | bytes 4194304 | tf_op jit(solution)/shard_map/params/pallas_call | solution.py:379
  87.6 7.2 %all-to-all-done.3 = f32[8,64,128]{2,1,0:T(8,128)S(1)} async-done(((f32[8,64,128]{2,1,0:T(8,128)}), f32[8,64,128]{2,1,0:T(8,128)S(1)}, u32[]{:S(2)}, u32[]{:S(2)}) %all-to-all-start.3) | async-done | bytes 262176 | tf_op jit(solution)/shard_map/all_to_all | solution.py:451
  94.8 5.6 %all-to-all-start.4 = ((f32[32,1,128]{2,1,0:T(1,128)}), f32[32,1,128]{2,1,0:T(1,128)S(1)}, u32[]{:S(2)}, u32[]{:S(2)}) async-start(f32[32,1,128]{2,1,0:T(1,128)} %get-tuple-element.42), calls=%async_computation.4 | async-start | bytes 32768 | tf_op jit(solution)/shard_map/all_to_all | solution.py:453
  100.4 1.9 %collective-permute-start.1 = (f32[512,128]{1,0:T(8,128)S(1)}, f32[512,128]{1,0:T(8,128)S(1)}, u32[]{:S(2)}, u32[]{:S(2)}) collective-permute-start(f32[512,128]{1,0:T(8,128)S(1)} %bitcast.11), channel_id=1, source_target_pairs={{0,1},{1,0},{2,3},{3,2},{4,5},{5,4},{6,7},{7,6},{8,9},{9,8},{10,11... | collective-permute-start | bytes 786440 | tf_op jit(solution)/shard_map/ppermute | solution.py:452
  102.3 2.7 %dx.1 = bf16[512,512]{1,0:T(8,128)(2,1)} custom-call(f32[32,1,4096]{2,1,0:T(1,128)S(1)} %all-to-all-done.1.refs_0_.got_ref, f32[512,512]{1,0:T(8,128)} %copy-done, bf16[512,128]{1,0:T(8,128)(2,1)} %refs_3_.7, f32[8,512]{1,0:T(8,128)} %refs_5_.3, f32[1,8]{1,0:T(1,128)} %bitcast.16, f32[1,8]{1,0:T(1,128)} %bitcast.20), custom_call_target="tpu_custom_call" | custom-call | flops 1073741824 | bytes 4194304 | tf_op jit(solution)/shard_map/dx/pallas_call | solution.py:379
  105.1 3.8 %all-to-all-done.4 = f32[32,1,128]{2,1,0:T(1,128)S(1)} async-done(((f32[32,1,128]{2,1,0:T(1,128)}), f32[32,1,128]{2,1,0:T(1,128)S(1)}, u32[]{:S(2)}, u32[]{:S(2)}) %all-to-all-start.4) | async-done | bytes 16416 | tf_op jit(solution)/shard_map/all_to_all | solution.py:453
  108.9 0.1 reduce_sum.9
  109.0 0.6 fusion
  109.6 0.0 collective-permute-done.1
  109.6 0.8 broadcast_select_fusion
  (1 shorter events, 0.0 us)
Async XLA Ops:
  31.7 21.5 %all-to-all-start.1 = ((f32[32,1,4096]{2,1,0:T(1,128)}), f32[32,1,4096]{2,1,0:T(1,128)S(1)}, u32[]{:S(2)}, u32[]{:S(2)}) async-start(f32[32,1,4096]{2,1,0:T(1,128)} %scan.1), calls=%async_computation.1 | async-start | bytes 1048576 | tf_op jit(solution)/shard_map/all_to_all | solution.py:443
  43.7 1.0 copy-start
  44.7 0.7 copy-start.1
  45.4 0.6 copy-start.2
  46.0 0.6 copy-start.3
  46.6 0.6 copy-start.4
  53.9 3.4 %collective-permute-start = (f32[512,128]{1,0:T(8,128)S(1)}, f32[512,128]{1,0:T(8,128)S(1)}, u32[]{:S(2)}, u32[]{:S(2)}) collective-permute-start(f32[512,128]{1,0:T(8,128)S(1)} %get-tuple-element.41), channel_id=1, source_target_pairs={{0,1},{1,0},{2,3},{3,2},{4,5},{5,4},{6,7},{7,6},{8,9},{9,8},{10,11... | collective-permute-start | bytes 786440 | tf_op jit(solution)/shard_map/ppermute | solution.py:446
  80.4 14.4 %all-to-all-start.3 = ((f32[8,64,128]{2,1,0:T(8,128)}), f32[8,64,128]{2,1,0:T(8,128)S(1)}, u32[]{:S(2)}, u32[]{:S(2)}) async-start(f32[8,64,128]{2,1,0:T(8,128)} %fold.1), calls=%async_computation.3 | async-start | bytes 524288 | tf_op jit(solution)/shard_map/all_to_all | solution.py:451
  94.8 14.1 %all-to-all-start.4 = ((f32[32,1,128]{2,1,0:T(1,128)}), f32[32,1,128]{2,1,0:T(1,128)S(1)}, u32[]{:S(2)}, u32[]{:S(2)}) async-start(f32[32,1,128]{2,1,0:T(1,128)} %get-tuple-element.42), calls=%async_computation.4 | async-start | bytes 32768 | tf_op jit(solution)/shard_map/all_to_all | solution.py:453
  100.4 9.2 %collective-permute-start.1 = (f32[512,128]{1,0:T(8,128)S(1)}, f32[512,128]{1,0:T(8,128)S(1)}, u32[]{:S(2)}, u32[]{:S(2)}) collective-permute-start(f32[512,128]{1,0:T(8,128)S(1)} %bitcast.11), channel_id=1, source_target_pairs={{0,1},{1,0},{2,3},{3,2},{4,5},{5,4},{6,7},{7,6},{8,9},{9,8},{10,11... | collective-permute-start | bytes 786440 | tf_op jit(solution)/shard_map/ppermute | solution.py:452

commit v4 on v3

--- a/solution.py
+++ b/solution.py
@@ -264,25 +264,21 @@
     )
 
 
-def k_proj(core_ref, got_ref, xh_ref, xl_ref, gh_ref, gl_ref, db_ref, dc_ref, keep_ref, send_ref):
+def k_proj(mine, core_ref, got_ref, xh_ref, xl_ref, gh_ref, gl_ref, db_ref, dc_ref, out_ref):
     def carried(state, hi_ref, lo_ref):
         sh, sl = split2(state)
         two = mm(hi_ref[...], jnp.concatenate([sh, sl], axis=0), NT)
         return two[:, :STATE] + two[:, STATE:] + mm(lo_ref[...], sh, NT)
 
-    dc = dc_ref[...] + carried(join(got_ref, 0), gh_ref, gl_ref)
-    db = db_ref[...] + carried(join(got_ref, 1), xh_ref, xl_ref)
-    first = core_ref[0] == 0
-
-    @pl.when(first)
+    for_b = (core_ref[0] == 0) if mine else (core_ref[0] != 0)
+
+    @pl.when(for_b)
     def _():
-        keep_ref[...] = db
-        send_ref[...] = dc
-
-    @pl.when(jnp.logical_not(first))
+        out_ref[...] = db_ref[...] + carried(join(got_ref, 1), xh_ref, xl_ref)
+
+    @pl.when(jnp.logical_not(for_b))
     def _():
-        keep_ref[...] = dc
-        send_ref[...] = db
+        out_ref[...] = dc_ref[...] + carried(join(got_ref, 0), gh_ref, gl_ref)
 
 
 def k_fold(got_ref, out_ref):
@@ -410,9 +406,10 @@
     return call(k_inner, "inner", (odd, *args), outs, 1 << 33, 1, scratch, [SMEM])
 
 
-def proj(*args):
-    outs = [shape((TOK, STATE)), shape((TOK, STATE))]
-    return call(k_proj, "proj", args, outs, 1 << 30, specs=[SMEM])
+def proj(mine, *args):
+    body = functools.partial(k_proj, mine)
+    name = "kept" if mine else "sent"
+    return call(body, name, args, [shape((TOK, STATE))], 1 << 30, specs=[SMEM])[0]
 
 
 def params(pieces, *args):
@@ -441,9 +438,10 @@
     got = lax.all_to_all(send, ctx, 0, 0)
     part, rs, cs, db, dc, xh, xl, gh, gl, sk, state = inner(odd, *data, skip)
     got = lax.all_to_all(scan(odd, got), ctx, 0, 0)
-    keep, send = proj(core, got, xh, xl, gh, gl, db, dc)
+    factors = (core, got, xh, xl, gh, gl, db, dc)
     swap = [(0, 1), (1, 0)]
-    mine = keep + lax.ppermute(send, "c", swap)
+    mine = lax.ppermute(proj(False, *factors), "c", swap)
+    mine = proj(True, *factors) + mine
     grad_raw, partial = params(pieces, got, *data, rs, cs, sk, state)
     ranks = lax.axis_size("z")
     mine = lax.all_to_all(mine.reshape(ranks, TOK // ranks, STATE), "z", 0, 0)

time: 111 us -> 111 us (level)
    pallas_call x7 -> x8, Pallas kernels: 18.2 us -> 18.4 us  [call(): pl.pallas_call(body, in_specs=specs, out_specs=[VMEM] * len(outs), out_sh...]
where the time goes in v4:
time: 111 us; the launch traced here: 110 us
  blocking collectives  49.5 us (45%)
  Pallas kernels  18.4 us (17%)
  starting transfers between devices  18.4 us (17%)
  waiting for transfers between devices  18 us (16%)
  local copies, waits for them, and re-layouts  4.06 us (4%)
    all_to_all x1, blocking collectives, on_device(): got = lax.all_to_all(send, ctx, 0, 0)  27.2 us
    all_to_all x1, blocking collectives, on_device(): mine = lax.all_to_all(mine.reshape(ranks, TOK // ranks, STATE), 'z', 0, 0)  22.3 us
    pallas_call x8, Pallas kernels, call(): pl.pallas_call(body, in_specs=specs, out_specs=[VMEM] * len(outs), out_sh...  18.4 us
    all_to_all x1, waiting for transfers between devices, on_device(): mine = lax.all_to_all(fold(mine), 'z', 0, 0).reshape(TOK, STATE)  7.22 us
    all_to_all x1, waiting for transfers between devices, on_device(): got = lax.all_to_all(scan(odd, got), ctx, 0, 0)  5.96 us
    all_to_all x1, starting transfers between devices, on_device(): got = lax.all_to_all(scan(odd, got), ctx, 0, 0)  5.57 us
    all_to_all x1, starting transfers between devices, on_device(): partial = jnp.sum(lax.all_to_all(partial, ctx, 0, 0), axis=(0, 1))  5.57 us
    all_to_all x1, waiting for transfers between devices, on_device(): partial = jnp.sum(lax.all_to_all(partial, ctx, 0, 0), axis=(0, 1))  3.83 us
  transfers between devices with their start and end apart: 5, of which 4 were waited for; matrix products, arithmetic and copies ran while one was open for 1% of the time, Pallas kernels for 12%

profile of v4, /device:TPU:2, one launch (start us, length us, event | category | flops | bytes accessed | tf_op | source)
XLA Modules:
  0.0 110.1 jit_solution(16750879149077369095)
XLA Ops:
  0.6 2.7 %states.1 = f32[32,1,4224]{2,1,0:T(1,128)S(1)} custom-call(bf16[512,512]{1,0:T(8,128)(2,1)} %refs_1_.5, bf16[512,512]{1,0:T(8,128)(2,1)} %refs_2_.7, bf16[512,128]{1,0:T(8,128)(2,1)} %refs_3_.7, bf16[512,128]{1,0:T(8,128)(2,1)} %refs_4_.5, f32[8,512]{1,0:T(8,128)} %refs_5_.3, f32[1,8]{1,0:T(1,128)} %bitcast.13, f32[1,8]{1,0:T(1,128)} %bitcast.17), custom_call_target="tpu_custom_call" | custom-call | flops 2147483648 | bytes 4194304 | tf_op jit(solution)/shard_map/states/pallas_call | solution.py:375
  3.3 27.2 %all_to_all.25.got_ref = f32[32,1,4224]{2,1,0:T(1,128)S(1)} all-to-all(f32[32,1,4224]{2,1,0:T(1,128)S(1)} %states.1), channel_id=1, replica_groups=mesh['y'=8,'x'=4,'z'=8,'c'=2] {'y','x'}, dimensions={0} | all-to-all | bytes 1081344 | tf_op jit(solution)/shard_map/all_to_all | solution.py:438
  30.6 1.1 scan.1
  31.7 5.6 %all-to-all-start.1 = ((f32[32,1,4096]{2,1,0:T(1,128)}), f32[32,1,4096]{2,1,0:T(1,128)S(1)}, u32[]{:S(2)}, u32[]{:S(2)}) async-start(f32[32,1,4096]{2,1,0:T(1,128)} %scan.1), calls=%async_computation.1 | async-start | bytes 1048576 | tf_op jit(solution)/shard_map/all_to_all | solution.py:440
  37.2 6.5 %inner.1 = (f32[512,512]{1,0:T(8,128)S(1)}, f32[8,512]{1,0:T(8,128)S(1)}, f32[8,512]{1,0:T(8,128)S(1)}, f32[512,128]{1,0:T(8,128)S(1)}, f32[512,128]{1,0:T(8,128...) custom-call(s32[1]{0:T(128)} %bitcast.2.odd_ref.refs_0_, ...), custom_call_target="tpu_custom_call" | custom-call | flops 8589934592 | bytes 4194304 | tf_op jit(solution)/shard_map/inner/pallas_call | solution.py:375
  43.7 0.0 copy-start
  43.7 1.0 copy-done
  44.7 0.0 copy-start.1
  44.7 0.7 copy-done.1
  45.4 0.0 copy-start.2
  45.4 0.6 copy-done.2
  46.0 0.0 copy-start.3
  46.0 0.6 copy-done.3
  46.6 0.0 copy-start.4
  46.6 0.6 copy-done.4
  47.2 6.0 %all-to-all-done.1.refs_0_.got_ref = f32[32,1,4096]{2,1,0:T(1,128)S(1)} async-done(((f32[32,1,4096]{2,1,0:T(1,128)}), f32[32,1,4096]{2,1,0:T(1,128)S(1)}, u32[]{:S(2)}, u32[]{:S(2)}) %all-to-all-start.1) | async-done | bytes 524320 | tf_op jit(solution)/shard_map/all_to_all | solution.py:440
  53.2 0.5 sent.1
  53.6 1.9 %collective-permute-start = (f32[512,128]{1,0:T(8,128)S(1)}, f32[512,128]{1,0:T(8,128)S(1)}, u32[]{:S(2)}, u32[]{:S(2)}) collective-permute-start(f32[512,128]{1,0:T(8,128)S(1)} %sent.1), channel_id=1, source_target_pairs={{0,1},{1,0},{2,3},{3,2},{4,5},{5,4},{6,7},{7,6},{8,9},{9,8},{10,11... | collective-permute-start | bytes 786440 | tf_op jit(solution)/shard_map/ppermute | solution.py:443
  55.6 0.5 kept.1
  56.0 1.0 collective-permute-done
  57.1 22.3 %all_to_all.26.got_ref = f32[8,64,128]{2,1,0:T(8,128)S(1)} all-to-all(f32[8,64,128]{2,1,0:T(8,128)S(1)} %bitcast.10), channel_id=1, replica_groups=mesh['y'=8,'x'=4,'z'=8,'c'=2] {'z'}, dimensions={0} | all-to-all | bytes 524288 | tf_op jit(solution)/shard_map/all_to_all | solution.py:447
  79.4 0.7 fold.1
  80.1 3.4 %all-to-all-start.3 = ((f32[8,64,128]{2,1,0:T(8,128)}), f32[8,64,128]{2,1,0:T(8,128)S(1)}, u32[]{:S(2)}, u32[]{:S(2)}) async-start(f32[8,64,128]{2,1,0:T(8,128)} %fold.1), calls=%async_computation.3 | async-start | bytes 524288 | tf_op jit(solution)/shard_map/all_to_all | solution.py:449
  83.5 3.8 %params.1 = (f32[8,512]{1,0:T(8,128)}, f32[32,1,128]{2,1,0:T(1,128)}) custom-call(f32[32,1,4096]{2,1,0:T(1,128)S(1)} %all-to-all-done.1.refs_0_.got_ref, bf16[512,512]{1,0:T(8,128)(2,1)} %refs_1_.5, bf16[512,512]{1,0:T(8,128)(2,1)} %refs_2_.7, bf16[512,128]{1,0:T(8,128)(2,1)} %refs_3_.7, bf16[512,128]{1,0:T(8,128)(2,1)} %refs_4_.5, f32[8,512]{1,0:T(8,128)} %refs_5_.3, ...), custom_call_target="tpu_custom_call" | custom-call | flops 1073741824 | bytes 4194304 | tf_op jit(solution)/shard_map/params/pallas_call | solution.py:375
  87.3 7.2 %all-to-all-done.3 = f32[8,64,128]{2,1,0:T(8,128)S(1)} async-done(((f32[8,64,128]{2,1,0:T(8,128)}), f32[8,64,128]{2,1,0:T(8,128)S(1)}, u32[]{:S(2)}, u32[]{:S(2)}) %all-to-all-start.3) | async-done | bytes 262176 | tf_op jit(solution)/shard_map/all_to_all | solution.py:449
  94.5 5.6 %all-to-all-start.4 = ((f32[32,1,128]{2,1,0:T(1,128)}), f32[32,1,128]{2,1,0:T(1,128)S(1)}, u32[]{:S(2)}, u32[]{:S(2)}) async-start(f32[32,1,128]{2,1,0:T(1,128)} %get-tuple-element.38), calls=%async_computation.4 | async-start | bytes 32768 | tf_op jit(solution)/shard_map/all_to_all | solution.py:451
  100.1 1.9 %collective-permute-start.1 = (f32[512,128]{1,0:T(8,128)S(1)}, f32[512,128]{1,0:T(8,128)S(1)}, u32[]{:S(2)}, u32[]{:S(2)}) collective-permute-start(f32[512,128]{1,0:T(8,128)S(1)} %bitcast.11), channel_id=1, source_target_pairs={{0,1},{1,0},{2,3},{3,2},{4,5},{5,4},{6,7},{7,6},{8,9},{9,8},{10,11... | collective-permute-start | bytes 786440 | tf_op jit(solution)/shard_map/ppermute | solution.py:450
  102.0 2.8 %dx.1 = bf16[512,512]{1,0:T(8,128)(2,1)} custom-call(f32[32,1,4096]{2,1,0:T(1,128)S(1)} %all-to-all-done.1.refs_0_.got_ref, f32[512,512]{1,0:T(8,128)} %copy-done, bf16[512,128]{1,0:T(8,128)(2,1)} %refs_3_.7, f32[8,512]{1,0:T(8,128)} %refs_5_.3, f32[1,8]{1,0:T(1,128)} %bitcast.16, f32[1,8]{1,0:T(1,128)} %bitcast.20), custom_call_target="tpu_custom_call" | custom-call | flops 1073741824 | bytes 4194304 | tf_op jit(solution)/shard_map/dx/pallas_call | solution.py:375
  104.8 3.8 %all-to-all-done.4 = f32[32,1,128]{2,1,0:T(1,128)S(1)} async-done(((f32[32,1,128]{2,1,0:T(1,128)}), f32[32,1,128]{2,1,0:T(1,128)S(1)}, u32[]{:S(2)}, u32[]{:S(2)}) %all-to-all-start.4) | async-done | bytes 16416 | tf_op jit(solution)/shard_map/all_to_all | solution.py:451
  108.6 0.1 reduce_sum.9
  108.7 0.6 fusion
  109.3 0.0 collective-permute-done.1
  109.3 0.8 broadcast_select_fusion
  (1 shorter events, 0.0 us)
Async XLA Ops:
  31.7 21.5 %all-to-all-start.1 = ((f32[32,1,4096]{2,1,0:T(1,128)}), f32[32,1,4096]{2,1,0:T(1,128)S(1)}, u32[]{:S(2)}, u32[]{:S(2)}) async-start(f32[32,1,4096]{2,1,0:T(1,128)} %scan.1), calls=%async_computation.1 | async-start | bytes 1048576 | tf_op jit(solution)/shard_map/all_to_all | solution.py:440
  43.7 1.0 copy-start
  44.7 0.7 copy-start.1
  45.4 0.6 copy-start.2
  46.0 0.6 copy-start.3
  46.6 0.6 copy-start.4
  53.6 3.4 %collective-permute-start = (f32[512,128]{1,0:T(8,128)S(1)}, f32[512,128]{1,0:T(8,128)S(1)}, u32[]{:S(2)}, u32[]{:S(2)}) collective-permute-start(f32[512,128]{1,0:T(8,128)S(1)} %sent.1), channel_id=1, source_target_pairs={{0,1},{1,0},{2,3},{3,2},{4,5},{5,4},{6,7},{7,6},{8,9},{9,8},{10,11... | collective-permute-start | bytes 786440 | tf_op jit(solution)/shard_map/ppermute | solution.py:443
  80.1 14.4 %all-to-all-start.3 = ((f32[8,64,128]{2,1,0:T(8,128)}), f32[8,64,128]{2,1,0:T(8,128)S(1)}, u32[]{:S(2)}, u32[]{:S(2)}) async-start(f32[8,64,128]{2,1,0:T(8,128)} %fold.1), calls=%async_computation.3 | async-start | bytes 524288 | tf_op jit(solution)/shard_map/all_to_all | solution.py:449
  94.5 14.1 %all-to-all-start.4 = ((f32[32,1,128]{2,1,0:T(1,128)}), f32[32,1,128]{2,1,0:T(1,128)S(1)}, u32[]{:S(2)}, u32[]{:S(2)}) async-start(f32[32,1,128]{2,1,0:T(1,128)} %get-tuple-element.38), calls=%async_computation.4 | async-start | bytes 32768 | tf_op jit(solution)/shard_map/all_to_all | solution.py:451
  100.1 9.2 %collective-permute-start.1 = (f32[512,128]{1,0:T(8,128)S(1)}, f32[512,128]{1,0:T(8,128)S(1)}, u32[]{:S(2)}, u32[]{:S(2)}) collective-permute-start(f32[512,128]{1,0:T(8,128)S(1)} %bitcast.11), channel_id=1, source_target_pairs={{0,1},{1,0},{2,3},{3,2},{4,5},{5,4},{6,7},{7,6},{8,9},{9,8},{10,11... | collective-permute-start | bytes 786440 | tf_op jit(solution)/shard_map/ppermute | solution.py:450
